TPU v7x, 32 devices: a whole 2x2x4 slice. The times are simulated.
32 devices in a mesh: dp: 16 (over z, x, core), tensor: 2 (over y).
Axes of the slice: x: 2, y: 2, z: 4, core: 2. Of those that a mesh axis runs over, the one named last changes fastest.
Arguments:
- small_rows: bfloat16 [32768, 192], P(('dp', 'tensor')), may hold values from -6 to 6
- large_rows: bfloat16 [32768, 384], P(('dp', 'tensor')), may hold values from -6 to 6
- patch_counts: int32 [2, 192], P(None, ('dp', 'tensor')), may hold values from 37 to 197, as said below
- small_cotangent: bfloat16 [32768, 192], P(('dp', 'tensor')), may hold values from -6 to 6
- large_cotangent: bfloat16 [32768, 384], P(('dp', 'tensor')), may hold values from -6 to 6
- small_heads_in: bfloat16 [192, 576], replicated, may hold values from -0.4375 to 0.4375
- small_heads_out: bfloat16 [192, 192], replicated, may hold values from -3.5 to 3.5
- small_up: bfloat16 [192, 768], P(None, 'tensor'), may hold values from -0.4375 to 0.4375
- small_up_bias: bfloat16 [768], P('tensor'), may hold values from -3 to 3
- small_down: bfloat16 [768, 192], P('tensor'), may hold values from -0.21875 to 0.21875
- large_heads_in: bfloat16 [384, 1152], replicated, may hold values from -0.3125 to 0.3125
- large_heads_out: bfloat16 [384, 384], replicated, may hold values from -2.5 to 2.5
- large_up: bfloat16 [384, 1536], P(None, 'tensor'), may hold values from -0.3125 to 0.3125
- large_up_bias: bfloat16 [1536], P('tensor'), may hold values from -3 to 3
- large_down: bfloat16 [1536, 384], P('tensor'), may hold values from -0.15625 to 0.15625
- small_cls_enter: bfloat16 [192, 384], replicated, may hold values from -0.4375 to 0.4375
- large_cross_in: bfloat16 [384, 1152], replicated, may hold values from -0.3125 to 0.3125
- large_cross_out: bfloat16 [384, 384], replicated, may hold values from -2.5 to 2.5
- small_cls_leave: bfloat16 [384, 192], replicated, may hold values from -0.3125 to 0.3125
- large_cls_enter: bfloat16 [384, 192], replicated, may hold values from -0.3125 to 0.3125
- small_cross_in: bfloat16 [192, 576], replicated, may hold values from -0.4375 to 0.4375
- small_cross_out: bfloat16 [192, 192], replicated, may hold values from -3.5 to 3.5
- large_cls_leave: bfloat16 [192, 384], replicated, may hold values from -0.4375 to 0.4375
- small_gains: bfloat16 [5, 192], replicated, may hold values from 0.099609375 to 1.8984375
- small_shifts: bfloat16 [14, 192], replicated, may hold values from -1.5 to 1.5
- large_gains: bfloat16 [5, 384], replicated, may hold values from 0.099609375 to 1.8984375
- large_shifts: bfloat16 [14, 384], replicated, may hold values from -1.5 to 1.5
Outputs:
- small_out: bfloat16 [32768, 192], P(('dp', 'tensor'))
- large_out: bfloat16 [32768, 384], P(('dp', 'tensor'))
- small_rows_grad: float32 [32768, 192], P(('dp', 'tensor'))
- large_rows_grad: float32 [32768, 384], P(('dp', 'tensor'))
- grad_small_heads_in: float32 [192, 576], replicated
- grad_small_heads_out: float32 [192, 192], replicated
- grad_small_up: float32 [192, 768], P(None, 'tensor')
- grad_small_up_bias: float32 [768], P('tensor')
- grad_small_down: float32 [768, 192], P('tensor')
- grad_large_heads_in: float32 [384, 1152], replicated
- grad_large_heads_out: float32 [384, 384], replicated
- grad_large_up: float32 [384, 1536], P(None, 'tensor')
- grad_large_up_bias: float32 [1536], P('tensor')
- grad_large_down: float32 [1536, 384], P('tensor')
- grad_small_cls_enter: float32 [192, 384], replicated
- grad_large_cross_in: float32 [384, 1152], replicated
- grad_large_cross_out: float32 [384, 384], replicated
- grad_small_cls_leave: float32 [384, 192], replicated
- grad_large_cls_enter: float32 [384, 192], replicated
- grad_small_cross_in: float32 [192, 576], replicated
- grad_small_cross_out: float32 [192, 192], replicated
- grad_large_cls_leave: float32 [192, 384], replicated
- grad_small_gains: float32 [5, 192], replicated
- grad_small_shifts: float32 [14, 192], replicated
- grad_large_gains: float32 [5, 384], replicated
- grad_large_shifts: float32 [14, 384], replicated
Inputs may be any that keep to these rules, and one draw needn't show every extreme that they name: `patch_counts`: each column is one crop, global or local: a global crop has 197 small and 145 large rows, a local one 37 and 65. Each run of 6 columns holds exactly 4 global crops, in drawn order, so the crops of one block take 4 * 197 + 2 * 37 small rows and 710 large rows.
All inputs are finite; a program needn't handle non-finite values.
Results may differ from a plain program's by a relative error of at most 0.024.
Values may be sent and summed in bfloat16 or wider, within the bound.
A program may use at most 256 MiB of HBM per device.

v0:
```python
import jax
import jax.numpy as jnp
from jax import lax
from jax.sharding import PartitionSpec as P

HEADS = 6
QBLK = 512
MARGIN = 256


NEGATIVE = -1e30
EPSILON = 1e-06


def layer_norm(values, gain, shift):
    center = values - jnp.mean(values, -1, keepdims=True)
    spread = jnp.mean(center * center, -1, keepdims=True)
    return center * lax.rsqrt(spread + EPSILON) * gain + shift


def smooth(values):
    return jax.nn.gelu(values, approximate=False)


def norm_smooth(values, gain, shift):
    return smooth(layer_norm(values, gain, shift))


def to_low(values):
    return values.astype(jnp.bfloat16)


def matmul(left, right):
    return jnp.dot(left, right, preferred_element_type=jnp.float32)


def contract_rows(left, right):
    return lax.dot_general(
        left, right, (((0,), (0,)), ((), ())), preferred_element_type=jnp.float32
    )


def contract_cols(left, right):
    return lax.dot_general(
        left, right, (((1,), (1,)), ((), ())), preferred_element_type=jnp.float32
    )


def norm_pullback(function, values, gain, shift, grad_result):
    unused, pullback = jax.vjp(function, values, gain, shift)
    return pullback(grad_result)


def crop_layout(lengths, row_count):
    crop_ends = jnp.cumsum(lengths)
    firsts = crop_ends - lengths
    places = jnp.arange(row_count, dtype=jnp.int32)
    segment = jnp.sum((places[:, None] >= crop_ends[None, :]).astype(jnp.int32), 1)
    return (segment, firsts)


def head_views(packed, segment):
    row_count = packed.shape[0]
    columns = packed.shape[1] // 3
    head_size = columns // HEADS
    window = min(row_count, QBLK + 2 * MARGIN)
    blocks = row_count // QBLK
    queries = packed[:, :columns].reshape(blocks, QBLK, HEADS, head_size)
    all_keys = packed[:, columns : 2 * columns].reshape(row_count, HEADS, head_size)
    all_values = packed[:, 2 * columns :].reshape(row_count, HEADS, head_size)
    offsets = jnp.clip(jnp.arange(blocks, dtype=jnp.int32) * QBLK - MARGIN, 0, row_count - window)
    return (
        queries,
        all_keys,
        all_values,
        segment.reshape(blocks, QBLK),
        offsets,
        window,
        float(head_size) ** (-0.5),
    )


def masked_scores(block_queries, block_segment, near_keys, near_segment, factor):
    scores = (
        jnp.einsum("qhd,khd->hqk", block_queries, near_keys, preferred_element_type=jnp.float32)
        * factor
    )
    return jnp.where((block_segment[:, None] == near_segment[None, :])[None], scores, NEGATIVE)


def attend_forward(packed, segment):
    queries, all_keys, all_values, block_segments, offsets, window, factor = head_views(
        packed, segment
    )

    def one_block(pieces):
        block_queries, block_segment, offset = pieces
        scores = masked_scores(block_queries, block_segment, all_keys, segment, factor)
        highest = jnp.max(scores, -1, keepdims=True)
        powers = jnp.exp(scores - highest)
        totals = jnp.sum(powers, -1, keepdims=True)
        chances = to_low(powers / totals)
        mixed = jnp.einsum("hqk,khd->qhd", chances, all_values, preferred_element_type=jnp.float32)
        return (mixed, (highest + jnp.log(totals))[:, :, 0])

    mixed, log_totals = lax.map(one_block, (queries, block_segments, offsets))
    return (to_low(mixed.reshape(packed.shape[0], -1)), log_totals)


def attend_backward(packed, segment, log_totals, grad_mixed):
    queries, all_keys, all_values, block_segments, offsets, window, factor = head_views(
        packed, segment
    )
    row_count = packed.shape[0]
    blocks = queries.shape[0]
    head_size = queries.shape[3]
    grad_blocks = grad_mixed.reshape(blocks, QBLK, HEADS, head_size)

    def one_block(carry, pieces):
        grad_keys, grad_values = carry
        block_queries, block_segment, offset, block_logs, block_grad = pieces
        scores = masked_scores(block_queries, block_segment, all_keys, segment, factor)
        chances = jnp.exp(scores - block_logs[:, :, None])
        low_chances = to_low(chances)
        grad_near_values = jnp.einsum(
            "hqk,qhd->khd", low_chances, block_grad, preferred_element_type=jnp.float32
        )
        grad_chances = jnp.einsum(
            "qhd,khd->hqk", block_grad, all_values, preferred_element_type=jnp.float32
        )
        inner = jnp.sum(grad_chances * chances, -1, keepdims=True)
        grad_scores = to_low(chances * (grad_chances - inner) * factor)
        grad_block_queries = jnp.einsum(
            "hqk,khd->qhd", grad_scores, all_keys, preferred_element_type=jnp.float32
        )
        grad_near_keys = jnp.einsum(
            "hqk,qhd->khd", grad_scores, block_queries, preferred_element_type=jnp.float32
        )
        grad_keys = grad_keys + grad_near_keys
        grad_values = grad_values + grad_near_values
        return ((grad_keys, grad_values), grad_block_queries)

    empty_grad = jnp.zeros((row_count, HEADS, head_size), jnp.float32)
    (grad_keys, grad_values), grad_queries = lax.scan(
        one_block,
        (empty_grad, empty_grad),
        (queries, block_segments, offsets, log_totals, grad_blocks),
    )
    return jnp.concatenate(
        [
            grad_queries.reshape(row_count, -1),
            grad_keys.reshape(row_count, -1),
            grad_values.reshape(row_count, -1),
        ],
        1,
    )


def mlp_forward(normed_mid, up_weight, up_bias, down_weight):
    gathered = lax.all_gather(normed_mid, "tensor", axis=0, tiled=True)
    hidden = matmul(gathered, up_weight) + up_bias
    active = to_low(smooth(hidden))
    mixed = lax.psum_scatter(matmul(active, down_weight), "tensor", scatter_dimension=0, tiled=True)
    kept = (gathered, hidden, active, up_weight, down_weight)
    return (mixed, kept)


def mlp_backward(grad_out, kept):
    inputs_kept, hidden, active, up_matrix, down_matrix = kept
    out_low = to_low(grad_out)
    grad_rows = lax.all_gather(out_low, "tensor", axis=0, tiled=True)
    unused, pullback = jax.vjp(smooth, hidden)
    grad_hidden = pullback(contract_cols(grad_rows, down_matrix))[0]
    grad_bias = jnp.sum(grad_hidden, 0)
    hidden_low = to_low(grad_hidden)
    grad_up = contract_rows(inputs_kept, hidden_low)
    grad_down = contract_rows(active, grad_rows)
    grad_normed = lax.psum_scatter(
        contract_cols(hidden_low, up_matrix).astype(jnp.bfloat16),
        "tensor",
        scatter_dimension=0,
        tiled=True,
    ).astype(jnp.float32)
    return (grad_normed, (grad_up, grad_bias, grad_down))


def block_forward(
    inputs, segment, gains, shifts, heads_in, heads_out, up_weight, up_bias, down_weight
):
    values = inputs.astype(jnp.float32)
    nothing = jnp.zeros(shifts.shape[1:], jnp.float32)
    normed_in = to_low(layer_norm(values, gains[0], shifts[0]))
    packed = to_low(matmul(normed_in, heads_in) + jnp.concatenate([shifts[1], nothing, shifts[2]]))
    attended, log_totals = attend_forward(packed, segment)
    middle = values + matmul(attended, heads_out) + shifts[3]
    normed_mid = to_low(layer_norm(middle, gains[1], shifts[4]))
    mixed, kept = mlp_forward(normed_mid, up_weight, up_bias, down_weight)
    result = middle + mixed + shifts[5]
    return (result, (values, normed_in, packed, log_totals, attended, middle, kept))


def block_backward(grad_out, saved, segment, gains, shifts, heads_in, heads_out):
    values, normed_in, packed, log_totals, attended, middle, kept = saved
    columns = values.shape[1]
    grad_normed_mid, column_grads = mlp_backward(grad_out, kept)
    grad_mid_norm, gain_mid, shift_mid = norm_pullback(
        layer_norm, middle, gains[1], shifts[4], grad_normed_mid
    )
    grad_middle = grad_out + grad_mid_norm
    middle_low = to_low(grad_middle)
    grad_heads_out = contract_rows(attended, middle_low)
    grad_attended = to_low(contract_cols(middle_low, heads_out))
    grad_packed = attend_backward(packed, segment, log_totals, grad_attended)
    query_bias = jnp.sum(grad_packed[:, :columns], 0)
    value_bias = jnp.sum(grad_packed[:, 2 * columns :], 0)
    packed_low = to_low(grad_packed)
    grad_heads_in = contract_rows(normed_in, packed_low)
    grad_in_norm, gain_in, shift_in = norm_pullback(
        layer_norm, values, gains[0], shifts[0], contract_cols(packed_low, heads_in)
    )
    grad_values = grad_middle + grad_in_norm
    block_gains = jnp.stack([gain_in, gain_mid])
    block_shifts = jnp.stack(
        [shift_in, query_bias, value_bias, jnp.sum(grad_middle, 0), shift_mid, jnp.sum(grad_out, 0)]
    )
    return (grad_values, grad_heads_in, grad_heads_out, column_grads, block_gains, block_shifts)


def split_cross(own_proj, row_proj, head_size):
    crops = own_proj.shape[0]
    columns = head_size * HEADS
    queries = own_proj[:, :columns].reshape(crops, HEADS, head_size)
    own_keys = own_proj[:, columns : 2 * columns].reshape(crops, HEADS, head_size)
    own_values = own_proj[:, 2 * columns :].reshape(crops, HEADS, head_size)
    row_keys = row_proj[:, :columns].reshape(-1, HEADS, head_size)
    row_values = row_proj[:, columns:].reshape(-1, HEADS, head_size)
    return (queries, own_keys, own_values, row_keys, row_values)


def cross_forward(
    cls_rows,
    other_rows,
    other_segment,
    other_firsts,
    gains_own,
    shifts_own,
    gains_other,
    shifts_other,
    weight_enter,
    weight_cross,
    weight_out,
    weight_leave,
):
    crops = cls_rows.shape[0]
    other_count = other_rows.shape[0]
    columns = other_rows.shape[1]
    head_size = columns // HEADS
    factor = float(head_size) ** (-0.5)
    nothing = jnp.zeros((columns,), jnp.float32)
    lifted = to_low(norm_smooth(cls_rows, gains_own[2], shifts_own[6]))
    moved = matmul(lifted, weight_enter) + shifts_other[8]
    query_norm = to_low(layer_norm(moved, gains_other[3], shifts_other[9]))
    key_norm = to_low(layer_norm(other_rows, gains_other[3], shifts_other[9]))
    own_proj = to_low(
        matmul(query_norm, weight_cross)
        + jnp.concatenate([shifts_other[10], nothing, shifts_other[11]])
    )
    row_proj = to_low(
        matmul(key_norm, weight_cross[:, columns:]) + jnp.concatenate([nothing, shifts_other[11]])
    )
    queries, own_keys, own_values, row_keys, row_values = split_cross(own_proj, row_proj, head_size)
    places = jnp.arange(other_count, dtype=jnp.int32)
    crop_ids = jnp.arange(crops, dtype=jnp.int32)
    usable = (other_segment[None, :] == crop_ids[:, None]) & (
        places[None, :] != other_firsts[:, None]
    )
    own_scores = jnp.sum(queries.astype(jnp.float32) * own_keys.astype(jnp.float32), -1) * factor
    row_scores = (
        jnp.einsum("chd,khd->chk", queries, row_keys, preferred_element_type=jnp.float32) * factor
    )
    row_scores = jnp.where(usable[:, None, :], row_scores, NEGATIVE)
    scores = jnp.concatenate([own_scores[:, :, None], row_scores], 2)
    highest = jnp.max(scores, -1, keepdims=True)
    powers = jnp.exp(scores - highest)
    chances = powers / jnp.sum(powers, -1, keepdims=True)
    low_chances = to_low(chances)
    mixed = low_chances[:, :, 0:1].astype(jnp.float32) * own_values.astype(
        jnp.float32
    ) + jnp.einsum(
        "chk,khd->chd", low_chances[:, :, 1:], row_values, preferred_element_type=jnp.float32
    )
    attended = to_low(mixed.reshape(crops, columns))
    joined = moved + matmul(attended, weight_out) + shifts_other[12]
    spread_out = to_low(norm_smooth(joined, gains_other[4], shifts_other[13]))
    new_cls = matmul(spread_out, weight_leave) + shifts_own[7]
    saved = (
        cls_rows,
        other_rows,
        lifted,
        moved,
        query_norm,
        key_norm,
        own_proj,
        row_proj,
        chances,
        attended,
        joined,
        spread_out,
    )
    return (new_cls, saved)


def cross_backward(
    grad_new,
    saved,
    gains_own,
    shifts_own,
    gains_other,
    shifts_other,
    weight_enter,
    weight_cross,
    weight_out,
    weight_leave,
):
    (
        cls_rows,
        other_rows,
        lifted,
        moved,
        query_norm,
        key_norm,
        own_proj,
        row_proj,
        chances,
        attended,
        joined,
        spread_out,
    ) = saved
    crops = cls_rows.shape[0]
    other_count = other_rows.shape[0]
    columns = other_rows.shape[1]
    head_size = columns // HEADS
    factor = float(head_size) ** (-0.5)
    leave_bias = jnp.sum(grad_new, 0)
    new_low = to_low(grad_new)
    grad_leave = contract_rows(spread_out, new_low)
    grad_joined, rln_gain, rln_shift = norm_pullback(
        norm_smooth, joined, gains_other[4], shifts_other[13], contract_cols(new_low, weight_leave)
    )
    out_bias = jnp.sum(grad_joined, 0)
    joined_low = to_low(grad_joined)
    grad_out = contract_rows(attended, joined_low)
    mixed_low = to_low(contract_cols(joined_low, weight_out)).reshape(crops, HEADS, head_size)
    grad_mixed = mixed_low.astype(jnp.float32)
    queries, own_keys, own_values, row_keys, row_values = split_cross(own_proj, row_proj, head_size)
    low_chances = to_low(chances)
    grad_own_values = low_chances[:, :, 0:1].astype(jnp.float32) * grad_mixed
    grad_row_values = jnp.einsum(
        "chk,chd->khd", low_chances[:, :, 1:], mixed_low, preferred_element_type=jnp.float32
    )
    grad_own_chance = jnp.sum(grad_mixed * own_values.astype(jnp.float32), -1)
    grad_row_chance = jnp.einsum(
        "chd,khd->chk", mixed_low, row_values, preferred_element_type=jnp.float32
    )
    grad_chances = jnp.concatenate([grad_own_chance[:, :, None], grad_row_chance], 2)
    inner = jnp.sum(grad_chances * chances, -1, keepdims=True)
    grad_scores = to_low(chances * (grad_chances - inner) * factor)
    own_grad_score = grad_scores[:, :, 0:1].astype(jnp.float32)
    grad_queries = own_grad_score * own_keys.astype(jnp.float32) + jnp.einsum(
        "chk,khd->chd", grad_scores[:, :, 1:], row_keys, preferred_element_type=jnp.float32
    )
    grad_own_keys = own_grad_score * queries.astype(jnp.float32)
    grad_row_keys = jnp.einsum(
        "chk,chd->khd", grad_scores[:, :, 1:], queries, preferred_element_type=jnp.float32
    )
    grad_own = jnp.concatenate(
        [
            grad_queries.reshape(crops, columns),
            grad_own_keys.reshape(crops, columns),
            grad_own_values.reshape(crops, columns),
        ],
        1,
    )
    grad_row_proj = jnp.concatenate(
        [
            grad_row_keys.reshape(other_count, columns),
            grad_row_values.reshape(other_count, columns),
        ],
        1,
    )
    query_bias = jnp.sum(grad_queries.reshape(crops, columns), 0)
    value_bias = jnp.sum(grad_own_values.reshape(crops, columns), 0) + jnp.sum(
        grad_row_values.reshape(other_count, columns), 0
    )
    own_low = to_low(grad_own)
    rows_low = to_low(grad_row_proj)
    grad_cross = contract_rows(query_norm, own_low) + jnp.concatenate(
        [jnp.zeros((columns, columns), jnp.float32), contract_rows(key_norm, rows_low)], 1
    )
    grad_moved_norm, cln_gain_query, cln_shift_query = norm_pullback(
        layer_norm, moved, gains_other[3], shifts_other[9], contract_cols(own_low, weight_cross)
    )
    grad_other, cln_gain_rows, cln_shift_rows = norm_pullback(
        layer_norm,
        other_rows,
        gains_other[3],
        shifts_other[9],
        contract_cols(rows_low, weight_cross[:, columns:]),
    )
    grad_moved = grad_joined + grad_moved_norm
    enter_bias = jnp.sum(grad_moved, 0)
    moved_low = to_low(grad_moved)
    grad_enter = contract_rows(lifted, moved_low)
    grad_cls, pln_gain, pln_shift = norm_pullback(
        norm_smooth, cls_rows, gains_own[2], shifts_own[6], contract_cols(moved_low, weight_enter)
    )
    query_gains = pln_gain[None]
    query_shifts = jnp.stack([pln_shift, leave_bias])
    key_gains = jnp.stack([cln_gain_query + cln_gain_rows, rln_gain])
    key_shifts = jnp.stack(
        [enter_bias, cln_shift_query + cln_shift_rows, query_bias, value_bias, out_bias, rln_shift]
    )
    return (
        grad_cls,
        grad_other,
        (grad_enter, grad_cross, grad_out, grad_leave),
        query_gains,
        query_shifts,
        key_gains,
        key_shifts,
    )


def shards(
    small_rows,
    large_rows,
    patch_counts,
    small_cotangent,
    large_cotangent,
    small_heads_in,
    small_heads_out,
    small_up,
    small_up_bias,
    small_down,
    large_heads_in,
    large_heads_out,
    large_up,
    large_up_bias,
    large_down,
    small_cls_enter,
    large_cross_in,
    large_cross_out,
    small_cls_leave,
    large_cls_enter,
    small_cross_in,
    small_cross_out,
    large_cls_leave,
    small_gains,
    small_shifts,
    large_gains,
    large_shifts,
):
    small_gain_table = small_gains.astype(jnp.float32)
    small_shift_table = small_shifts.astype(jnp.float32)
    large_gain_table = large_gains.astype(jnp.float32)
    large_shift_table = large_shifts.astype(jnp.float32)
    small_segment, small_firsts = crop_layout(patch_counts[0], small_rows.shape[0])
    large_segment, large_firsts = crop_layout(patch_counts[1], large_rows.shape[0])
    small_block, small_saved = block_forward(
        small_rows,
        small_segment,
        small_gain_table,
        small_shift_table,
        small_heads_in,
        small_heads_out,
        small_up,
        small_up_bias,
        small_down,
    )
    large_block, large_saved = block_forward(
        large_rows,
        large_segment,
        large_gain_table,
        large_shift_table,
        large_heads_in,
        large_heads_out,
        large_up,
        large_up_bias,
        large_down,
    )
    small_new, small_cross_kept = cross_forward(
        jnp.take(small_block, small_firsts, axis=0),
        large_block,
        large_segment,
        large_firsts,
        small_gain_table,
        small_shift_table,
        large_gain_table,
        large_shift_table,
        small_cls_enter,
        large_cross_in,
        large_cross_out,
        small_cls_leave,
    )
    large_new, large_cross_kept = cross_forward(
        jnp.take(large_block, large_firsts, axis=0),
        small_block,
        small_segment,
        small_firsts,
        large_gain_table,
        large_shift_table,
        small_gain_table,
        small_shift_table,
        large_cls_enter,
        small_cross_in,
        small_cross_out,
        large_cls_leave,
    )
    small_out = small_block.at[small_firsts].set(small_new).astype(jnp.bfloat16)
    large_out = large_block.at[large_firsts].set(large_new).astype(jnp.bfloat16)
    small_grad = small_cotangent.astype(jnp.float32)
    large_grad = large_cotangent.astype(jnp.float32)
    small_back = cross_backward(
        jnp.take(small_grad, small_firsts, axis=0),
        small_cross_kept,
        small_gain_table,
        small_shift_table,
        large_gain_table,
        large_shift_table,
        small_cls_enter,
        large_cross_in,
        large_cross_out,
        small_cls_leave,
    )
    large_back = cross_backward(
        jnp.take(large_grad, large_firsts, axis=0),
        large_cross_kept,
        large_gain_table,
        large_shift_table,
        small_gain_table,
        small_shift_table,
        large_cls_enter,
        small_cross_in,
        small_cross_out,
        large_cls_leave,
    )
    small_grad = (
        small_grad.at[small_firsts].set(0.0).at[small_firsts].add(small_back[0]) + large_back[1]
    )
    large_grad = (
        large_grad.at[large_firsts].set(0.0).at[large_firsts].add(large_back[0]) + small_back[1]
    )
    grad_small_cls_enter, grad_large_cross_in, grad_large_cross_out, grad_small_cls_leave = (
        small_back[2]
    )
    grad_large_cls_enter, grad_small_cross_in, grad_small_cross_out, grad_large_cls_leave = (
        large_back[2]
    )
    (
        large_rows_grad,
        grad_large_heads_in,
        grad_large_heads_out,
        large_column_grads,
        large_block_gains,
        large_block_shifts,
    ) = block_backward(
        large_grad,
        large_saved,
        large_segment,
        large_gain_table,
        large_shift_table,
        large_heads_in,
        large_heads_out,
    )
    grad_large_up, grad_large_up_bias, grad_large_down = large_column_grads
    grad_large_gains = jnp.concatenate([large_block_gains, large_back[3], small_back[5]], 0)
    grad_large_shifts = jnp.concatenate([large_block_shifts, large_back[4], small_back[6]], 0)
    (
        small_rows_grad,
        grad_small_heads_in,
        grad_small_heads_out,
        small_column_grads,
        small_block_gains,
        small_block_shifts,
    ) = block_backward(
        small_grad,
        small_saved,
        small_segment,
        small_gain_table,
        small_shift_table,
        small_heads_in,
        small_heads_out,
    )
    grad_small_up, grad_small_up_bias, grad_small_down = small_column_grads
    grad_small_gains = jnp.concatenate([small_block_gains, small_back[3], large_back[5]], 0)
    grad_small_shifts = jnp.concatenate([small_block_shifts, small_back[4], large_back[6]], 0)
    (
        grad_small_heads_in,
        grad_small_heads_out,
        grad_large_heads_in,
        grad_large_heads_out,
        grad_small_cls_enter,
        grad_large_cross_in,
        grad_large_cross_out,
        grad_small_cls_leave,
        grad_large_cls_enter,
        grad_small_cross_in,
        grad_small_cross_out,
        grad_large_cls_leave,
        grad_small_gains,
        grad_small_shifts,
        grad_large_gains,
        grad_large_shifts,
    ) = lax.psum(
        (
            grad_small_heads_in,
            grad_small_heads_out,
            grad_large_heads_in,
            grad_large_heads_out,
            grad_small_cls_enter,
            grad_large_cross_in,
            grad_large_cross_out,
            grad_small_cls_leave,
            grad_large_cls_enter,
            grad_small_cross_in,
            grad_small_cross_out,
            grad_large_cls_leave,
            grad_small_gains,
            grad_small_shifts,
            grad_large_gains,
            grad_large_shifts,
        ),
        ("dp", "tensor"),
    )
    (
        grad_small_up,
        grad_small_up_bias,
        grad_small_down,
        grad_large_up,
        grad_large_up_bias,
        grad_large_down,
    ) = lax.psum(
        (
            grad_small_up,
            grad_small_up_bias,
            grad_small_down,
            grad_large_up,
            grad_large_up_bias,
            grad_large_down,
        ),
        "dp",
    )
    return (
        small_out,
        large_out,
        small_rows_grad,
        large_rows_grad,
        grad_small_heads_in,
        grad_small_heads_out,
        grad_small_up,
        grad_small_up_bias,
        grad_small_down,
        grad_large_heads_in,
        grad_large_heads_out,
        grad_large_up,
        grad_large_up_bias,
        grad_large_down,
        grad_small_cls_enter,
        grad_large_cross_in,
        grad_large_cross_out,
        grad_small_cls_leave,
        grad_large_cls_enter,
        grad_small_cross_in,
        grad_small_cross_out,
        grad_large_cls_leave,
        grad_small_gains,
        grad_small_shifts,
        grad_large_gains,
        grad_large_shifts,
    )


def solution(mesh):
    return jax.shard_map(
        shards,
        mesh=mesh,
        in_specs=(
            P(("dp", "tensor"), None),
            P(("dp", "tensor"), None),
            P(None, ("dp", "tensor")),
            P(("dp", "tensor"), None),
            P(("dp", "tensor"), None),
            P(),
            P(),
            P(None, "tensor"),
            P("tensor"),
            P("tensor", None),
            P(),
            P(),
            P(None, "tensor"),
            P("tensor"),
            P("tensor", None),
            P(),
            P(),
            P(),
            P(),
            P(),
            P(),
            P(),
            P(),
            P(),
            P(),
            P(),
            P(),
        ),
        out_specs=(
            P(("dp", "tensor"), None),
            P(("dp", "tensor"), None),
            P(("dp", "tensor"), None),
            P(("dp", "tensor"), None),
            P(),
            P(),
            P(None, "tensor"),
            P("tensor"),
            P("tensor", None),
            P(),
            P(),
            P(None, "tensor"),
            P("tensor"),
            P("tensor", None),
            P(),
            P(),
            P(),
            P(),
            P(),
            P(),
            P(),
            P(),
            P(),
            P(),
            P(),
            P(),
        ),
        check_vma=False,
    )
```

profile of v0, /device:TPU:0, one launch (start us, length us, event | category | flops | bytes accessed | tf_op | source)
XLA Modules:
  0.0 977.0 jit_solution(14216733083545266941)
XLA Ops:
  22.2 23.6 %while.59 = (s32[]{:T(128)}, bf16[2,512,6,64]{1,3,2,0:T(8,128)(2,1)}, f32[2,6,512]{2,1,0:T(8,128)S(1)}, s32[2,512]{1,0:T(2,128)S(1)}, s32[1024]{0:T(1024)S(1)}, ...) while((s32[]{:T(128)}, ...), condition=%wide.region_23.25_spmd.clone, body=%wide.region_20.24_spmd.sunk.clone | while | flops 843576320 | bytes 52164800 | solution.py:106
  25.0 3.6 fusion.603
  28.7 4.4 fusion.604
  36.8 3.6 fusion.603
  40.5 4.4 fusion.604
  55.9 21.8 %while.58 = (s32[]{:T(128)}, bf16[2,512,6,32]{1,3,2,0:T(8,128)(2,1)S(1)}, f32[2,6,512]{2,1,0:T(8,128)S(1)}, s32[2,512]{1,0:T(2,128)S(1)}, s32[1024]{0:T(1024)S(1...) while((s32[]{:T(128)}, ...), condition=%wide.region_7.8_spmd.clone, body=%wide.region_4.0_spmd.sunk.clone | while | flops 440923136 | bytes 41351276 | solution.py:106
  58.9 3.7 fusion.598
  62.6 4.2 fusion.599
  69.8 3.7 fusion.598
  73.5 4.2 fusion.599
  79.4 12.7 %all_gather.12 = bf16[2048,192]{0,1:T(8,128)(2,1)S(1)} all-gather(bf16[1024,192]{0,1:T(8,128)(2,1)S(1)} %add_convert_fusion.6), channel_id=1, replica_groups=mesh['dp'=16,'tensor'=2] {'tensor'}, dimensions={0}, use_global_device_ids=true | all-gather | bytes 1179648 | tf_op jit(solution)/shard_map/all_gather | solution.py:160
  92.2 8.8 multiply_convert_fusion.3
  104.2 17.6 %multiply_convert_fusion.2 = (bf16[2048,768]{1,0:T(8,128)(2,1)S(1)}, f32[2048,768]{1,0:T(8,128)}, f32[2048,768]{1,0:T(8,128)}) fusion(f32[768]{0:T(1024)S(1)} %convert_element_type.310, bf16[2048,384]{0,1:T(8,128)(2,1)} %all-gather.3.cloned.1.call-done, bf16[384,768]{1,0:T(8,128)(2,1)S(1)} %copy-done.324), kind=kOutput, calls=%fused_computation.145 | convolution fusion | flops 1311768576 | bytes 17894400 | tf_op jit(solution)/shard_map/dot_general | solution.py:34
  134.4 10.0 %scatter_custom_fusion.4 = f32[1024,384]{1,0:T(8,128)S(1)} fusion(f32[1024,384]{1,0:T(8,128)S(1)} %convert_element_type.337, s32[6]{0:T(128)S(1)} %get-tuple-element.896, f32[]{:T(128)} %constant.110.clone.1), kind=kCustom, calls=%fused_computation.520 | custom fusion | bytes 1572868 | tf_op jit(solution)/shard_map/scatter | solution.py:551
  162.2 15.3 %reduce-scatter.7.cloned.1.call-done = f32[1024,384]{0,1:T(8,128)} async-done(((f32[2048,384]{0,1:T(8,128)}), f32[1024,384]{0,1:T(8,128)}) %reduce-scatter.7.cloned.1.call-update) | async-done | bytes 1572880 | tf_op jit(solution)/shard_map/reduce_scatter | solution.py:163
  177.6 3.4 fusion.403
  314.6 14.3 %all_gather.14 = bf16[2048,192]{1,0:T(8,128)(2,1)S(1)} all-gather(bf16[1024,192]{1,0:T(8,128)(2,1)S(1)} %get-tuple-element.844), channel_id=1, replica_groups=mesh['dp'=16,'tensor'=2] {'tensor'}, dimensions={0}, use_global_device_ids=true | all-gather | bytes 1179648 | tf_op jit(solution)/shard_map/all_gather | solution.py:171
  334.0 4.3 fusion.432
  349.3 3.4 scatter_custom_fusion.5
  378.2 18.9 %all-gather.5.cloned.1.call-done = bf16[2048,384]{1,0:T(8,128)(2,1)} async-done(((bf16[1024,384]{1,0:T(8,128)(2,1)}), bf16[2048,384]{1,0:T(8,128)(2,1)}) %all-gather.5.cloned.1.call-update) | async-done | bytes 1572880 | tf_op jit(solution)/shard_map/all_gather | solution.py:171
  397.1 8.4 fusion.430
  410.0 152.7 %while.60 = (s32[]{:T(128)}, f32[1024,6,32]{0,2,1:T(8,128)}, f32[1024,6,32]{0,2,1:T(8,128)}, f32[2,512,6,32]{1,3,2,0:T(8,128)}, bf16[2,512,6,32]{1,3,2,0:T(8,128...) while((s32[]{:T(128)}, f32[1024,6,32]{0,2,1:T(8,128)}, ...), condition=%wide.region_67.70_spmd.clone.clone, body=%wide.region_65.69_spmd.clone.sunk.clone | while | flops 1089740800 | bytes 147179696 | solution.py:144
  410.2 6.5 fusion.615
  416.7 6.3 fusion.616
  423.4 29.1 %fusion.617 = f32[1024,6,32]{0,2,1:T(8,128)} fusion(f32[6,512,1024]{2,1,0:T(8,128)} %fusion.615, f32[6,512,1024]{2,1,0:T(8,128)} %fusion.616, f32[6,512]{1,0:T(8,128)S(1)} %dynamic-slice_bitcast_fusion.6, pred[512,1024]{1,0:T(8,128)(4,1)S(1)} %broadcast_compare_fusion.14, f32[1024,6,32]{0,2,1:T(8,128)} %get-tuple-element.1348, ...), kind=kOutput, calls=%fused_computation.64.clone.1.clone | convolution fusion | flops 236326912 | bytes 53182468 | tf_op jit(solution)/shard_map/while/body/eval_jaxpr/hqk,qhd->khd/dot_general | solution.py:136
  452.6 7.2 fusion.618
  459.8 26.3 %fusion.619 = f32[2,512,6,32]{1,3,2,0:T(8,128)} fusion(f32[2,512,6,32]{1,3,2,0:T(8,128)} %get-tuple-element.1350, s32[]{:T(128)S(6)} %copy.485, bf16[1024,6,32]{0,2,1:T(8,128)(2,1)S(1)} %get-tuple-element.1365, f32[6,512,1024]{2,1,0:T(8,128)} %fusion.615, f32[6,512,1024]{2,1,0:T(8,128)} %fusion.616, ...), kind=kOutput, calls=%fused_computation.67.clone.1.clone | convolution fusion | flops 235933696 | bytes 52199428 | tf_op jit(solution)/shard_map/while/body/eval_jaxpr/hqk,khd->qhd/dot_general | solution.py:133
  486.1 6.4 fusion.615
  492.5 6.3 fusion.616
  499.1 29.4 %fusion.617 = f32[1024,6,32]{0,2,1:T(8,128)} fusion(f32[6,512,1024]{2,1,0:T(8,128)} %fusion.615, f32[6,512,1024]{2,1,0:T(8,128)} %fusion.616, f32[6,512]{1,0:T(8,128)S(1)} %dynamic-slice_bitcast_fusion.6, pred[512,1024]{1,0:T(8,128)(4,1)S(1)} %broadcast_compare_fusion.14, f32[1024,6,32]{0,2,1:T(8,128)} %get-tuple-element.1348, ...), kind=kOutput, calls=%fused_computation.64.clone.1.clone | convolution fusion | flops 236326912 | bytes 53182468 | tf_op jit(solution)/shard_map/while/body/eval_jaxpr/hqk,qhd->khd/dot_general | solution.py:136
  528.6 7.4 fusion.618
  536.0 26.3 %fusion.619 = f32[2,512,6,32]{1,3,2,0:T(8,128)} fusion(f32[2,512,6,32]{1,3,2,0:T(8,128)} %get-tuple-element.1350, s32[]{:T(128)S(6)} %copy.485, bf16[1024,6,32]{0,2,1:T(8,128)(2,1)S(1)} %get-tuple-element.1365, f32[6,512,1024]{2,1,0:T(8,128)} %fusion.615, f32[6,512,1024]{2,1,0:T(8,128)} %fusion.616, ...), kind=kOutput, calls=%fused_computation.67.clone.1.clone | convolution fusion | flops 235933696 | bytes 52199428 | tf_op jit(solution)/shard_map/while/body/eval_jaxpr/hqk,khd->qhd/dot_general | solution.py:133
  592.3 176.6 %while.61 = (s32[]{:T(128)}, f32[1024,6,64]{0,2,1:T(8,128)}, f32[1024,6,64]{0,2,1:T(8,128)}, f32[2,512,6,64]{1,3,2,0:T(8,128)}, bf16[2,512,6,64]{1,3,2,0:T(8,128...) while((s32[]{:T(128)}, f32[1024,6,64]{0,2,1:T(8,128)}, ...), condition=%wide.region_83.86_spmd.clone.clone, body=%wide.region_81.85_spmd.clone.sunk.clone | while | flops 2097160192 | bytes 152680624 | solution.py:144
  592.4 7.4 fusion.630
  599.8 6.3 fusion.631
  607.3 29.5 %bitcast_add_fusion.6 = f32[1024,6,64]{0,2,1:T(8,128)} fusion(f32[1024,6,64]{0,2,1:T(8,128)} %get-tuple-element.1381, f32[6,512,1024]{2,1,0:T(8,128)} %fusion.630, f32[6,512,1024]{2,1,0:T(8,128)} %fusion.631, f32[6,512]{1,0:T(8,128)S(1)} %dynamic-slice_bitcast_fusion.7, pred[512,1024]{1,0:T(8,128)(4,1)} %broadcast_compare_fusion.15, ...), kind=kOutput, calls=%fused_computation.112.clone.1.clone | convolution fusion | flops 438046720 | bytes 54951940 | tf_op jit(solution)/shard_map/while/body/eval_jaxpr/hqk,qhd->khd/dot_general | solution.py:136
  636.9 9.3 bitcast_add_fusion.7
  646.2 33.9 %fusion.632 = f32[2,512,6,64]{1,3,2,0:T(8,128)} fusion(f32[2,512,6,64]{1,3,2,0:T(8,128)} %get-tuple-element.1383, s32[]{:T(128)S(6)} %copy.499, bf16[1024,6,64]{0,2,1:T(8,128)(2,1)S(1)} %get-tuple-element.1398, f32[6,512,1024]{2,1,0:T(8,128)} %fusion.630, f32[6,512,1024]{2,1,0:T(8,128)} %fusion.631, ...), kind=kOutput, calls=%fused_computation.114.clone.1.clone | convolution fusion | flops 437260288 | bytes 52985860 | tf_op jit(solution)/shard_map/while/body/eval_jaxpr/hqk,khd->qhd/dot_general | solution.py:133
  680.1 7.4 fusion.630
  687.5 6.3 fusion.631
  694.9 30.0 %bitcast_add_fusion.6 = f32[1024,6,64]{0,2,1:T(8,128)} fusion(f32[1024,6,64]{0,2,1:T(8,128)} %get-tuple-element.1381, f32[6,512,1024]{2,1,0:T(8,128)} %fusion.630, f32[6,512,1024]{2,1,0:T(8,128)} %fusion.631, f32[6,512]{1,0:T(8,128)S(1)} %dynamic-slice_bitcast_fusion.7, pred[512,1024]{1,0:T(8,128)(4,1)} %broadcast_compare_fusion.15, ...), kind=kOutput, calls=%fused_computation.112.clone.1.clone | convolution fusion | flops 438046720 | bytes 54951940 | tf_op jit(solution)/shard_map/while/body/eval_jaxpr/hqk,qhd->khd/dot_general | solution.py:136
  725.0 9.8 %bitcast_add_fusion.7 = f32[1024,6,64]{0,2,1:T(8,128)} fusion(f32[1024,6,64]{0,2,1:T(8,128)} %get-tuple-element.1382, f32[6,512,1024]{2,1,0:T(8,128)} %fusion.631, f32[6,512]{1,0:T(8,128)S(1)} %dynamic-slice_bitcast_fusion.7, pred[512,1024]{1,0:T(8,128)(4,1)} %broadcast_compare_fusion.15, pred[]{:T(512)S(6)} %compare.13, ...), kind=kOutput, calls=%fused_computation.111.clone.1.clone | convolution fusion | flops 416022528 | bytes 16658437 | tf_op jit(solution)/shard_map/while/body/eval_jaxpr/hqk,qhd->khd/dot_general | solution.py:125
  734.8 33.9 %fusion.632 = f32[2,512,6,64]{1,3,2,0:T(8,128)} fusion(f32[2,512,6,64]{1,3,2,0:T(8,128)} %get-tuple-element.1383, s32[]{:T(128)S(6)} %copy.499, bf16[1024,6,64]{0,2,1:T(8,128)(2,1)S(1)} %get-tuple-element.1398, f32[6,512,1024]{2,1,0:T(8,128)} %fusion.630, f32[6,512,1024]{2,1,0:T(8,128)} %fusion.631, ...), kind=kOutput, calls=%fused_computation.114.clone.1.clone | convolution fusion | flops 437260288 | bytes 52985860 | tf_op jit(solution)/shard_map/while/body/eval_jaxpr/hqk,khd->qhd/dot_general | solution.py:133
  783.3 3.3 scatter_fusion.1
  795.6 35.7 %all-reduce.6 = (f32[384]{0:T(512)}, f32[768]{0:T(1024)}) all-reduce(f32[384]{0:T(512)S(1)} %copy-done.297, f32[768]{0:T(1024)S(1)} %copy-done.275), channel_id=1, replica_groups=mesh['dp'=16,'tensor'=2] {'dp'}, use_global_device_ids=true, to_apply=%region_90.93 | all-reduce | flops 1152 | bytes 9216 | tf_op jit(solution)/shard_map/psum | solution.py:642
  833.6 4.3 fusion.431
  846.2 38.6 %all-reduce.4 = (f32[5,192]{1,0:T(8,128)}, f32[14,192]{1,0:T(8,128)}, f32[5,384]{1,0:T(8,128)}, f32[14,384]{1,0:T(8,128)}) all-reduce(f32[5,192]{1,0:T(8,128)S(1)} %concatenate.90, f32[14,192]{1,0:T(8,128)S(1)} %concatenate.91, f32[5,384]{1,0:T(8,128)S(1)} %concatenate.92, ...), channel_id=1, replica_groups=mesh['dp'=16,'tensor'=2] {'dp','tensor'}, use_global_device_ids=true, to_apply=%region_112.115 | all-reduce | flops 10944 | bytes 87552 | tf_op jit(solution)/shard_map/psum | solution.py:614
  884.8 67.4 %all-reduce.11.cloned.1.call-done = (f32[192,576]{1,0:T(8,128)}, f32[192,192]{1,0:T(8,128)}, f32[384,1152]{1,0:T(8,128)}, f32[384,384]{1,0:T(8,128)}, f32[192,38...) async-done(((f32[192,576]{1,0:T(8,128)}, ...) | async-done | bytes 7077904 | tf_op jit(solution)/shard_map/psum | solution.py:614
  (1076 shorter events, 333.8 us)
Async XLA Ops:
  7.2 97.0 %all-gather.3.cloned.1.call-start = ((), (), s32[]{:S(2)}) async-start(), calls=%async_computation.5 | async-start | bytes 2359296 | tf_op jit(solution)/shard_map/all_gather | solution.py:160
  12.0 36.5 %copy-start.9 = (bf16[1024,384]{0,1:T(8,128)(2,1)}, bf16[1024,384]{0,1:T(8,128)(2,1)S(1)}, u32[]{:S(2)}) copy-start(bf16[1024,384]{0,1:T(8,128)(2,1)S(1)} %copy.332) | copy-start | bytes 2359300
  13.4 36.3 %copy-start.160 = (f32[384]{0:T(512)}, f32[384]{0:T(512)S(1)}, u32[]{:S(2)}) copy-start(f32[384]{0:T(512)S(1)} %get-tuple-element.686) | copy-start | bytes 4612
  51.6 95.2 %reduce-scatter.5.cloned.1.call-start = ((), (), s32[]{:S(2)}) async-start(), calls=%async_computation.4 | async-start | bytes 2359296 | tf_op jit(solution)/shard_map/reduce_scatter | solution.py:163
  53.9 25.3 %copy-start.193 = (f32[1,192]{1,0:T(1,128)}, f32[1,192]{1,0:T(1,128)S(1)}, u32[]{:S(2)}) copy-start(f32[1,192]{1,0:T(1,128)S(1)} %get-tuple-element.886) | copy-start | bytes 2308
  55.9 22.4 %copy-start.304 = (bf16[384]{0:T(512)(128)(2,1)S(1)}, bf16[384]{0:T(512)(128)(2,1)}, u32[]{:S(2)}) copy-start(bf16[384]{0:T(512)(128)(2,1)} %param.47) | copy-start | bytes 2308
  55.9 22.4 %copy-start.86 = (bf16[192,192]{1,0:T(8,128)(2,1)S(1)}, bf16[192,192]{1,0:T(8,128)(2,1)}, u32[]{:S(2)}) copy-start(bf16[192,192]{1,0:T(8,128)(2,1)} %param.45) | copy-start | bytes 221188
  77.8 14.4 %copy-start.7 = (bf16[1024,6,32]{0,2,1:T(8,128)(2,1)}, bf16[1024,6,32]{0,2,1:T(8,128)(2,1)S(1)}, u32[]{:S(2)}) copy-start(bf16[1024,6,32]{0,2,1:T(8,128)(2,1)S(1)} %get-tuple-element.1467) | copy-start | bytes 1179652
  77.8 14.4 %copy-start.22 = (bf16[1024,6,32]{0,2,1:T(8,128)(2,1)}, bf16[1024,6,32]{0,2,1:T(8,128)(2,1)S(1)}, u32[]{:S(2)}) copy-start(bf16[1024,6,32]{0,2,1:T(8,128)(2,1)S(1)} %get-tuple-element.1470) | copy-start | bytes 1179652
  79.0 21.9 %copy-start.118 = (f32[1024]{0:T(1024)}, f32[1024]{0:T(1024)S(1)}, u32[]{:S(2)}) copy-start(f32[1024]{0:T(1024)S(1)} %broadcast_multiply_fusion.4) | copy-start | bytes 12292
  79.2 21.8 %copy-start.179 = (f32[1024]{0:T(1024)}, f32[1024]{0:T(1024)S(1)}, u32[]{:S(2)}) copy-start(f32[1024]{0:T(1024)S(1)} %multiply_reduce_fusion.9) | copy-start | bytes 12292
  79.2 21.8 %copy-start.148 = (f32[1024]{0:T(1024)}, f32[1024]{0:T(1024)S(1)}, u32[]{:S(2)}) copy-start(f32[1024]{0:T(1024)S(1)} %fusion.330) | copy-start | bytes 12292
  104.1 73.4 %reduce-scatter.7.cloned.1.call-start = ((), (), s32[]{:S(2)}) async-start(), calls=%async_computation.6 | async-start | bytes 4718592 | tf_op jit(solution)/shard_map/reduce_scatter | solution.py:163
  104.2 17.7 %copy-start.273 = (f32[768]{0:T(1024)}, f32[768]{0:T(1024)S(1)}, u32[]{:S(2)}) copy-start(f32[768]{0:T(1024)S(1)} %convert_element_type.310) | copy-start | bytes 9220
  104.2 19.4 %copy-start.322 = (bf16[768,384]{1,0:T(8,128)(2,1)S(1)}, bf16[768,384]{1,0:T(8,128)(2,1)}, u32[]{:S(2)}) copy-start(bf16[768,384]{1,0:T(8,128)(2,1)} %param.53) | copy-start | bytes 1769476
  126.8 244.0 %reduce-scatter.9.cloned.1.call-start = ((), (), s32[]{:S(2)}) async-start(), calls=%async_computation.7 | async-start | bytes 1179648 | tf_op jit(solution)/shard_map/reduce_scatter | solution.py:178
  128.5 24.2 %copy-start.198 = (pred[6]{0:T(512)(128)(4,1)}, pred[6]{0:T(512)(128)(4,1)S(1)}, u32[]{:S(2)}) copy-start(pred[6]{0:T(512)(128)(4,1)S(1)} %get-tuple-element.898) | copy-start | bytes 22
  128.5 55.4 %copy-start.205 = (pred[6]{0:T(512)(128)(4,1)}, pred[6]{0:T(512)(128)(4,1)S(1)}, u32[]{:S(2)}) copy-start(pred[6]{0:T(512)(128)(4,1)S(1)} %get-tuple-element.813) | copy-start | bytes 22
  129.7 14.7 %copy-start.288 = (s32[6]{0:T(128)}, s32[6]{0:T(128)S(1)}, u32[]{:S(2)}) copy-start(s32[6]{0:T(128)S(1)} %get-tuple-element.896) | copy-start | bytes 76
  131.9 14.9 %copy-start.269 = (f32[1,192]{1,0:T(1,128)S(1)}, f32[1,192]{1,0:T(1,128)}, u32[]{:S(2)}) copy-start(f32[1,192]{1,0:T(1,128)} %get-tuple-element.877) | copy-start | bytes 2308
  150.3 27.2 %copy-start.4 = (f32[1024,384]{0,1:T(8,128)S(1)}, f32[1024,384]{0,1:T(8,128)}, u32[]{:S(2)}) copy-start(f32[1024,384]{0,1:T(8,128)} %copy-done.3) | copy-start | bytes 4718596
  150.3 27.2 %copy-start.231 = (f32[384]{0:T(512)S(1)}, f32[384]{0:T(512)}, u32[]{:S(2)}) copy-start(f32[384]{0:T(512)} %get-tuple-element.664) | copy-start | bytes 4612
  152.2 28.7 %copy-start.96 = (f32[6,192]{1,0:T(8,128)}, f32[6,192]{1,0:T(8,128)S(1)}, u32[]{:S(2)}) copy-start(f32[6,192]{1,0:T(8,128)S(1)} %gather_fusion) | copy-start | bytes 13828
  153.9 27.0 %copy-start.76 = (f32[6,384]{1,0:T(8,128)}, f32[6,384]{1,0:T(8,128)S(1)}, u32[]{:S(2)}) copy-start(f32[6,384]{1,0:T(8,128)S(1)} %get-tuple-element.916) | copy-start | bytes 27652
  154.2 26.8 %copy-start.232 = (f32[6]{0:T(128)}, f32[6]{0:T(128)S(1)}, u32[]{:S(2)}) copy-start(f32[6]{0:T(128)S(1)} %fusion.351) | copy-start | bytes 76
  156.7 24.2 %copy-start.109 = (bf16[6,6,64]{2,1,0:T(8,128)(2,1)}, bf16[6,6,64]{2,1,0:T(8,128)(2,1)S(1)}, u32[]{:S(2)}) copy-start(bf16[6,6,64]{2,1,0:T(8,128)(2,1)S(1)} %reshape.1043) | copy-start | bytes 13828
  156.8 24.1 %copy-start.105 = (f32[6,6,64]{2,1,0:T(8,128)}, f32[6,6,64]{2,1,0:T(8,128)S(1)}, u32[]{:S(2)}) copy-start(f32[6,6,64]{2,1,0:T(8,128)S(1)} %reshape.1087) | copy-start | bytes 27652
  158.2 22.8 %copy-start.150 = (f32[1024]{0:T(1024)}, f32[1024]{0:T(1024)S(1)}, u32[]{:S(2)}) copy-start(f32[1024]{0:T(1024)S(1)} %broadcast_multiply_fusion.3) | copy-start | bytes 12292
  159.4 21.6 %copy-start.183 = (f32[1024]{0:T(1024)}, f32[1024]{0:T(1024)S(1)}, u32[]{:S(2)}) copy-start(f32[1024]{0:T(1024)S(1)} %multiply_reduce_fusion.8) | copy-start | bytes 12292
  159.4 21.5 %copy-start.168 = (f32[1024]{0:T(1024)}, f32[1024]{0:T(1024)S(1)}, u32[]{:S(2)}) copy-start(f32[1024]{0:T(1024)S(1)} %fusion.334) | copy-start | bytes 12292
  190.1 35.5 %copy-start.6 = (f32[1024,384]{0,1:T(8,128)S(1)}, f32[1024,384]{0,1:T(8,128)}, u32[]{:S(2)}) copy-start(f32[1024,384]{0,1:T(8,128)} %get-tuple-element.818) | copy-start | bytes 4718596
  267.3 14.5 %copy-start.95 = (f32[6,384]{1,0:T(8,128)S(1)}, f32[6,384]{1,0:T(8,128)}, u32[]{:S(2)}) copy-start(f32[6,384]{1,0:T(8,128)} %copy-done.94) | copy-start | bytes 27652
  267.4 20.1 %copy-start.83 = (bf16[6,6,1025]{2,0,1:T(8,128)(2,1)S(1)}, bf16[6,6,1025]{2,0,1:T(8,128)(2,1)}, u32[]{:S(2)}) copy-start(bf16[6,6,1025]{2,0,1:T(8,128)(2,1)} %copy-done.82) | copy-start | bytes 221404
  267.4 20.0 %copy-start.106 = (f32[6,6,64]{2,1,0:T(8,128)S(1)}, f32[6,6,64]{2,1,0:T(8,128)}, u32[]{:S(2)}) copy-start(f32[6,6,64]{2,1,0:T(8,128)} %copy-done.105) | copy-start | bytes 27652
  267.4 22.7 %copy-start.77 = (f32[6,384]{1,0:T(8,128)S(1)}, f32[6,384]{1,0:T(8,128)}, u32[]{:S(2)}) copy-start(f32[6,384]{1,0:T(8,128)} %copy-done.76) | copy-start | bytes 27652
  267.4 22.6 %copy-start.133 = (f32[384]{0:T(512)S(1)}, f32[384]{0:T(512)}, u32[]{:S(2)}) copy-start(f32[384]{0:T(512)} %get-tuple-element.688) | copy-start | bytes 4612
  268.6 26.6 %copy-start.97 = (f32[6,192]{1,0:T(8,128)S(1)}, f32[6,192]{1,0:T(8,128)}, u32[]{:S(2)}) copy-start(f32[6,192]{1,0:T(8,128)} %copy-done.96) | copy-start | bytes 13828
  289.6 17.4 %copy-start.112 = (bf16[6,6,64]{2,1,0:T(8,128)(2,1)S(1)}, bf16[6,6,64]{2,1,0:T(8,128)(2,1)}, u32[]{:S(2)}) copy-start(bf16[6,6,64]{2,1,0:T(8,128)(2,1)} %reshape.1058) | copy-start | bytes 13828
  306.9 22.1 %copy-start.330 = (f32[2048,384]{1,0:T(8,128)S(1)}, f32[2048,384]{1,0:T(8,128)}, u32[]{:S(2)}) copy-start(f32[2048,384]{1,0:T(8,128)} %get-tuple-element.904) | copy-start | bytes 9437188
  308.8 20.2 %copy-start.121 = (bf16[384,192]{0,1:T(8,128)(2,1)S(1)}, bf16[384,192]{0,1:T(8,128)(2,1)}, u32[]{:S(2)}) copy-start(bf16[384,192]{0,1:T(8,128)(2,1)} %param.48) | copy-start | bytes 442372
  308.8 20.2 %copy-start.329 = (f32[2048,384]{1,0:T(8,128)S(1)}, f32[2048,384]{1,0:T(8,128)}, u32[]{:S(2)}) copy-start(f32[2048,384]{1,0:T(8,128)} %get-tuple-element.824) | copy-start | bytes 9437188
  334.0 63.1 %all-gather.5.cloned.1.call-start = ((), (), s32[]{:S(2)}) async-start(), calls=%async_computation.8 | async-start | bytes 2359296 | tf_op jit(solution)/shard_map/all_gather | solution.py:171
  369.7 205.9 %reduce-scatter.11.cloned.1.call-start = ((), (), s32[]{:S(2)}) async-start(), calls=%async_computation.9 | async-start | bytes 2359296 | tf_op jit(solution)/shard_map/reduce_scatter | solution.py:178
  372.6 24.5 %copy-start.274 = (f32[768]{0:T(1024)S(1)}, f32[768]{0:T(1024)}, u32[]{:S(2)}) copy-start(f32[768]{0:T(1024)} %copy-done.273) | copy-start | bytes 9220
  372.6 24.5 %copy-start.323 = (bf16[768,384]{1,0:T(8,128)(2,1)S(1)}, bf16[768,384]{1,0:T(8,128)(2,1)}, u32[]{:S(2)}) copy-start(bf16[768,384]{1,0:T(8,128)(2,1)} %param.53) | copy-start | bytes 1769476
  409.9 474.9 %all-reduce.13.cloned.1.call-start = ((), (), s32[]{:S(2)}) async-start(), calls=%async_computation.11 | async-start | bytes 5898240 | tf_op jit(solution)/shard_map/psum | solution.py:642
  575.6 376.6 %all-reduce.11.cloned.1.call-start = ((), (), s32[]{:S(2)}) async-start(), calls=%async_computation.10 | async-start | bytes 14548992 | tf_op jit(solution)/shard_map/psum | solution.py:614
  791.2 40.1 %copy-start.29 = (f32[1024,192]{0,1:T(8,128)S(1)}, f32[1024,192]{0,1:T(8,128)}, u32[]{:S(2)}) copy-start(f32[1024,192]{0,1:T(8,128)} %copy-done.27) | copy-start | bytes 2359300
  (294 other events, 1404.6 us)
Sparse Core Ops, SparseCore 0:
  51.7 29.8 all-gather.2
  104.2 27.5 reduce-scatter.4
  134.1 43.3 reduce-scatter.6
  334.1 17.4 reduce-scatter.8
  369.9 27.1 all-gather.4
  410.0 26.0 reduce-scatter.10
  575.7 103.5 all-reduce.12
  777.1 175.0 all-reduce.10
where the time goes:
time: 990 us; the launch traced here: 977 us
  matrix products  493 us (50%)
  local copies, waits for them, and re-layouts  147 us (15%)
  other arithmetic  113 us (11%)
  waiting for transfers between devices  102 us (10%)
  blocking collectives  101 us (10%)
  between operations  18.2 us (2%)
    dot_general x4, matrix products, one_block(): jnp.einsum('hqk,khd->qhd', grad_scores, all_keys, preferred_element_type=...  120 us
    dot_general x4, matrix products, one_block(): jnp.einsum('hqk,qhd->khd', grad_scores, block_queries, preferred_element_...  118 us
    psum x1, waiting for transfers between devices, shards(): lax.psum((grad_small_heads_in, grad_small_heads_out, grad_large_heads_in,...  67.4 us
    unnamed x682, local copies, waits for them, and re-layouts  47.6 us
    dot_general x18, matrix products, matmul(): return jnp.dot(left, right, preferred_element_type=jnp.float32)  46.3 us
    dot_general x18, matrix products, contract_cols(): lax.dot_general(left, right, (((1,), (1,)), ((), ())), preferred_element_...  45.6 us
    psum x1, blocking collectives, shards(): lax.psum((grad_small_heads_in, grad_small_heads_out, grad_large_heads_in,...  38.6 us
    psum x1, blocking collectives, shards(): lax.psum((grad_small_up, grad_small_up_bias, grad_small_down, grad_large_...  35.7 us
  transfers between devices with their start and end apart: 8, of which 3 were waited for; matrix products, arithmetic and copies ran while one was open for 54% of the time, Pallas kernels for 0%

commit v1 on v0

v1 whole, which is shorter than its diff:
```python
import functools
import collections
import jax
import jax.numpy as jnp
from jax import lax
from jax.experimental import pallas as pl
from jax.experimental.pallas import tpu as pltpu
from jax.sharding import PartitionSpec as P

HEADS = 6
VMEM_LIMIT = 64 * 1024 * 1024
NEGATIVE = -1e30
EPSILON = 1e-06
F32, BF16 = jnp.float32, jnp.bfloat16
LANES = 384
CLS = 16
STACK = HEADS * CLS

GLOBAL_ROWS, LOCAL_ROWS = (197, 145), (37, 65)
LOG2E = 1.4426950408889634


def low(values):
    return values.astype(BF16)


def dot(left, right, left_axis, right_axis):
    return lax.dot_general(
        left, right, (((left_axis,), (right_axis,)), ((), ())), preferred_element_type=F32
    )


def nn(left, right):
    return dot(left, right, 1, 0)


def nt(left, right):
    return dot(left, right, 1, 1)


def tn(left, right):
    return dot(left, right, 0, 0)


class Branch:
    def __init__(self, index, rows, columns, hidden, width, layout):
        self.index, self.rows, self.columns, self.hidden = index, rows, columns, hidden
        self.head = columns // HEADS
        self.width, self.slots = width, len(layout)
        self.tokens = width * self.slots
        self.pieces = []
        self.bounds = []
        g_rows, l_rows = GLOBAL_ROWS[index], LOCAL_ROWS[index]
        for slot, crops in enumerate(layout):
            lane, ends = 0, []
            for crop in crops:
                length = g_rows if crop < 4 else l_rows if crop < 6 else rows - 4 * g_rows - 2 * l_rows
                self.pieces.append((slot * width + lane, length, crop))
                lane += length
                ends.append(lane)
            assert lane <= width
            self.bounds.append(ends)


def norm(values, axis):
    center = values - jnp.mean(values, axis, keepdims=True)
    scale = lax.rsqrt(jnp.mean(center * center, axis, keepdims=True) + EPSILON)
    return center * scale, scale


def norm_back(grad, unit, scale, axis):
    return scale * (
        grad
        - jnp.mean(grad, axis, keepdims=True)
        - unit * jnp.mean(grad * unit, axis, keepdims=True)
    )


def smooth_parts(values):
    chance = 0.5 + 0.5 * lax.erf(values * (0.5**0.5))
    slope = chance + values * (jnp.exp(values * values * -0.5) * 0.3989422804014327)
    return values * chance, slope


def pick(at, values):
    result = values[-1]
    for place in range(len(values) - 2, -1, -1):
        result = jnp.where(at == place, values[place], result)
    return result


def iota(shape, axis):
    return lax.broadcasted_iota(jnp.int32, shape, axis)


def slot_columns(branch, slot):
    return pl.ds(pl.multiple_of(slot * branch.width, branch.width), branch.width)


def places(counts, b):
    starts = [jnp.int32(0)] * 7
    begin, globals_seen, locals_seen = jnp.int32(0), jnp.int32(0), jnp.int32(0)
    for crop in range(6):
        rows = counts[b.index, crop]
        is_global = counts[0, crop] == GLOBAL_ROWS[0]
        for k in range(4):
            starts[k] = jnp.where(is_global & (globals_seen == k), begin, starts[k])
        for k in range(2):
            starts[4 + k] = jnp.where((~is_global) & (locals_seen == k), begin, starts[4 + k])
        begin = begin + rows
        globals_seen = globals_seen + jnp.where(is_global, 1, 0)
        locals_seen = locals_seen + jnp.where(is_global, 0, 1)
    starts[6] = begin
    return starts


def lay_out(b, r, counts):
    starts = places(counts, b)
    lane = iota((1, b.tokens), 1)
    source = jnp.full((1, b.tokens), -1, jnp.int32)
    patch = jnp.full((1, b.tokens), -1, jnp.int32)
    cls = jnp.full((1, b.tokens), -1, jnp.int32)
    for first, length, crop in b.pieces:
        inside = (lane >= first) & (lane < first + length)
        source = jnp.where(inside, lane - first + starts[crop], source)
        if crop < 6:
            patch = jnp.where(inside & (lane > first), crop, patch)
            cls = jnp.where(lane == first, crop, cls)
    r.index[0:1, :] = source
    r.index[1:2, :] = patch
    r.index[2:3, :] = cls
    at = iota((CLS, 1), 0)
    first_rows = jnp.full((CLS, 1), -1, jnp.int32)
    for crop in range(6):
        first_rows = jnp.where(at == crop, starts[crop], first_rows)
    chosen = low((iota((CLS, b.rows), 1) == first_rows).astype(F32))
    r.cot_cls[...] = nn(chosen, r.cot[...])


def bring_in(b, r):
    r.stack[0 : b.columns, :] = r.rows[...].T
    r.stack[b.columns : 2 * b.columns, :] = r.cot[...].T

    def body(slot, carry):
        cols = slot_columns(b, slot)
        chosen = low((iota((b.rows, b.width), 0) == r.index[0:1, cols]).astype(F32))
        both = nn(r.stack[...], chosen)
        r.x[:, cols] = low(both[: b.columns])
        keep = r.index[2:3, cols] < 0
        r.cotT[:, cols] = low(jnp.where(keep, both[b.columns :], 0.0))
        return carry

    lax.fori_loop(0, b.slots, body, 0)


def slot_mask(b, slot):
    ends = [pick(slot, [e[min(i, len(e) - 1)] for e in b.bounds]) for i in range(3)]

    def segment(axis):
        at = iota((b.width, b.width), axis)
        total = jnp.zeros((b.width, b.width), jnp.int32)
        for end in ends:
            total = total + (at >= end).astype(jnp.int32)
        return total

    return jnp.where(segment(0) == segment(1), 0.0, NEGATIVE)


def forward_attention(b, r):
    columns, head, width = b.columns, b.head, b.width
    factor = float(head) ** (-0.5) * LOG2E

    def body(slot, carry):
        cols = slot_columns(b, slot)
        x = r.x[:, cols].astype(F32)
        unit, scale = norm(x, 0)
        a = low(unit * r.gainT[:, 0:1] + r.shiftT[:, 0:1])
        r.a[0:columns, cols] = a
        nothing = jnp.zeros((columns, 1), F32)
        bias = jnp.concatenate([r.shiftT[:, 1:2], nothing, r.shiftT[:, 2:3]], 0)
        r.qkv[:, cols] = low(nn(r.w_inT[...], a) + bias)
        mask = slot_mask(b, slot)
        for h in range(HEADS):
            q = r.qkv[h * head : (h + 1) * head, cols]
            k = r.qkv[columns + h * head : columns + (h + 1) * head, cols]
            v = r.qkv[2 * columns + h * head : 2 * columns + (h + 1) * head, cols]
            scores = tn(k, q) * factor + mask
            highest = jnp.max(scores, 0, keepdims=True)
            powers = jnp.exp2(scores - highest)
            total = jnp.sum(powers, 0, keepdims=True)
            r.logs[h : h + 1, cols] = highest + jnp.log2(total)
            chances = low(powers * (1.0 / total))
            r.o[h * head : (h + 1) * head, cols] = low(nn(v, chances))
        y = x + nn(r.w_outT[...], r.o[0:columns, cols]) + r.shiftT[:, 3:4]
        r.y[:, cols] = y
        unit, scale = norm(y, 0)
        r.c[0:columns, cols] = low(unit * r.gainT[:, 1:2] + r.shiftT[:, 4:5])
        return carry

    lax.fori_loop(0, b.slots, body, 0)


def forward_mlp(b, r):
    chunk = 256 if b.hidden % 512 == 0 else b.hidden // 4
    r.cls[...] = jnp.zeros_like(r.cls)

    def body(slot, carry):
        cols = slot_columns(b, slot)
        c = r.c[0 : b.columns, cols]
        for at in range(0, b.hidden, chunk):
            hidden = nn(r.w_upT[at : at + chunk, :], c) + r.up_biasT[at : at + chunk, 0:1]
            active, slope = smooth_parts(hidden)
            r.u[at : at + chunk, cols] = low(active)
            r.g[at : at + chunk, cols] = low(slope)
        z = r.y[:, cols] + nn(r.w_downT[...], r.u[0 : b.hidden, cols]) + r.shiftT[:, 5:6]
        r.z[:, cols] = z
        z_low = low(z)
        r.out[:, cols] = z_low
        chosen = low((iota((CLS, b.width), 0) == r.index[2:3, cols]).astype(F32))
        r.cls[...] += nt(chosen, z_low) + nt(chosen, low(z - z_low.astype(F32)))
        unit, scale = norm(z, 0)
        r.n[:, cols] = low(unit * r.gainT[:, 3:4] + r.shiftT[:, 9:10])
        return carry

    lax.fori_loop(0, b.slots, body, 0)


def head_mask(columns):
    head = columns // HEADS
    at = iota((STACK, columns), 1)
    first = iota((STACK, columns), 0) // CLS * head
    return (at >= first) & (at < first + head)


def spread(values, mask):
    return jnp.where(mask, jnp.concatenate([values] * HEADS, 0), 0.0)


def gather_heads(values, mask):
    values = jnp.where(mask, values, 0.0)
    total = values[0:CLS]
    for h in range(1, HEADS):
        total = total + values[h * CLS : (h + 1) * CLS]
    return total


def column_sum(values):
    return jnp.sum(values, 0, keepdims=True)


def cross(b, r, o, ro, g):
    wide = o.columns
    factor = float(o.head) ** (-0.5)
    mask = head_mask(wide)
    og, ob = ro.gains, ro.shifts

    def row(table, at):
        return table[at : at + 1, :].astype(F32)

    xc = r.cls[...]
    unit2, scale2 = norm(xc, 1)
    lifted, slope2 = smooth_parts(unit2 * row(r.gains, 2) + row(r.shifts, 6))
    lifted = low(lifted)
    moved = nn(lifted, r.enter[...]) + row(ob, 8)
    unit3, scale3 = norm(moved, 1)
    query_norm = low(unit3 * row(og, 3) + row(ob, 9))
    q = low(nn(query_norm, ro.cross_in[:, 0:wide]) + row(ob, 10))
    own_k = low(nn(query_norm, ro.cross_in[:, wide : 2 * wide]))
    own_v = low(nn(query_norm, ro.cross_in[:, 2 * wide : 3 * wide]) + row(ob, 11))
    q_all = spread(q.astype(F32), mask)
    k_all = spread(own_k.astype(F32), mask)
    v_all = spread(own_v.astype(F32), mask)
    key_map = low(nt(low(q_all), ro.cross_in[:, wide : 2 * wide]))
    own_score = jnp.sum(q_all * k_all, 1, keepdims=True) * factor
    usable = ro.index[1:2, :] == iota((STACK, o.tokens), 0) % CLS
    scores = jnp.where(usable, nn(key_map, ro.n[...]) * factor, NEGATIVE)
    highest = jnp.maximum(own_score, jnp.max(scores, 1, keepdims=True))
    powers = jnp.exp(scores - highest)
    own_power = jnp.exp(own_score - highest)
    inverse = 1.0 / (own_power + jnp.sum(powers, 1, keepdims=True))
    chances = powers * inverse
    own_chance = own_power * inverse
    chances_low = low(chances)
    own_low = low(own_chance).astype(F32)
    ro.sp[STACK : 2 * STACK, :] = chances_low
    total = jnp.sum(chances_low.astype(F32), 1, keepdims=True)
    mean_row = low(nt(chances_low, ro.n[...]))
    value_bias = row(ob, 11)
    mixed = own_low * v_all + nn(mean_row, ro.cross_in[:, 2 * wide : 3 * wide]) + total * value_bias
    attended = low(gather_heads(mixed, mask))
    joined = moved + nn(attended, ro.cross_out[...]) + row(ob, 12)
    unit4, scale4 = norm(joined, 1)
    spread_out, slope4 = smooth_parts(unit4 * row(og, 4) + row(ob, 13))
    spread_out = low(spread_out)
    r.new_cls[...] = low(nn(spread_out, r.leave[...]) + row(r.shifts, 7))

    new_grad = r.cot_cls[...]
    new_low = low(new_grad)
    r.table[5 + 7 : 5 + 8, :] = column_sum(new_grad)
    g.leave(tn(spread_out, new_low))
    back = nt(new_low, r.leave[...]) * slope4
    ro.table[4:5, :] = column_sum(back * unit4)
    ro.table[5 + 13 : 5 + 14, :] = column_sum(back)
    joined_grad = norm_back(back * row(og, 4), unit4, scale4, 1)
    ro.table[5 + 12 : 5 + 13, :] = column_sum(joined_grad)
    joined_low = low(joined_grad)
    g.cross_out(tn(attended, joined_low))
    mixed_grad = low(nt(joined_low, ro.cross_out[...])).astype(F32)
    mixed_all = spread(mixed_grad, mask)
    mixed_all_low = low(mixed_all)
    own_v_grad = gather_heads(own_low * mixed_all, mask)
    own_chance_grad = jnp.sum(mixed_all * v_all, 1, keepdims=True)
    value_map = low(nt(mixed_all_low, ro.cross_in[:, 2 * wide : 3 * wide]))
    chance_grad = nn(value_map, ro.n[...]) + jnp.sum(mixed_all * value_bias, 1, keepdims=True)
    inner = own_chance_grad * own_chance + jnp.sum(chance_grad * chances, 1, keepdims=True)
    score_grad = low(chances * (chance_grad - inner) * factor)
    own_score_grad = low(own_chance * (own_chance_grad - inner) * factor).astype(F32)
    ro.sp[0:STACK, :] = score_grad
    mean_back = low(nt(score_grad, ro.n[...]))
    q_grad = gather_heads(
        own_score_grad * k_all + nn(mean_back, ro.cross_in[:, wide : 2 * wide]), mask
    )
    own_k_grad = gather_heads(own_score_grad * q_all, mask)
    ro.table[5 + 10 : 5 + 11, :] = column_sum(q_grad)
    ro.table[5 + 11 : 5 + 12, :] = column_sum(own_v_grad) + column_sum(total * mixed_all)
    q_low, k_low, v_low = low(q_grad), low(own_k_grad), low(own_v_grad)
    g.cross_in(
        0,
        tn(query_norm, q_low),
    )
    g.cross_in(
        1,
        tn(
            jnp.concatenate([query_norm, mean_back], 0),
            jnp.concatenate([k_low, low(q_all)], 0),
        ),
    )
    g.cross_in(
        2,
        tn(
            jnp.concatenate([query_norm, mean_row], 0),
            jnp.concatenate([v_low, mixed_all_low], 0),
        ),
    )
    back = (
        nt(q_low, ro.cross_in[:, 0:wide])
        + nt(k_low, ro.cross_in[:, wide : 2 * wide])
        + nt(v_low, ro.cross_in[:, 2 * wide : 3 * wide])
    )
    ro.table[3:4, :] = column_sum(back * unit3)
    ro.table[5 + 9 : 5 + 10, :] = column_sum(back)
    moved_grad = joined_grad + norm_back(back * row(og, 3), unit3, scale3, 1)
    ro.table[5 + 8 : 5 + 9, :] = column_sum(moved_grad)
    moved_low = low(moved_grad)
    g.enter(tn(lifted, moved_low))
    back = nt(moved_low, r.enter[...]) * slope2
    r.table[2:3, :] = column_sum(back * unit2)
    r.table[5 + 6 : 5 + 7, :] = column_sum(back)
    r.cls_grad[...] = norm_back(back * row(r.gains, 2), unit2, scale2, 1)
    ro.maps[0:STACK, :] = key_map
    ro.maps[STACK : 2 * STACK, :] = value_map


def backward_cross(b, r):
    r.sums[...] = jnp.zeros_like(r.sums)
    maps = r.maps[...].astype(F32).T.astype(BF16)
    cls_grad = r.cls_grad[...]
    high = low(cls_grad)
    pair = jnp.concatenate([high, low(cls_grad - high.astype(F32))], 0)

    def body(slot, carry):
        cols = slot_columns(b, slot)
        z = r.z[:, cols]
        unit, scale = norm(z, 0)
        grad = nn(maps, r.sp[:, cols])
        ones = jnp.ones((16, b.width), BF16)
        r.sums[0] += nt(ones, low(grad))
        r.sums[1] += nt(ones, low(grad * unit))
        chosen = low((iota((CLS, b.width), 0) == r.index[2:3, cols]).astype(F32))
        scatter = tn(pair, jnp.concatenate([chosen, chosen], 0))
        grad = norm_back(grad * r.gainT[:, 3:4], unit, scale, 0)
        r.z[:, cols] = r.cotT[:, cols].astype(F32) + scatter + grad
        return carry

    lax.fori_loop(0, b.slots, body, 0)
    r.table[3:4, :] += r.sums[1, 0:1, :]
    r.table[5 + 9 : 5 + 10, :] += r.sums[0, 0:1, :]


def put_out(b, r):
    def replace(slot, carry):
        cols = slot_columns(b, slot)
        cls = r.index[2:3, cols]
        chosen = low((iota((CLS, b.width), 0) == cls).astype(F32))
        new = low(tn(r.new_cls[...], chosen))
        r.out[:, cols] = jnp.where(cls >= 0, new.astype(F32), r.out[:, cols].astype(F32)).astype(BF16)
        return carry

    lax.fori_loop(0, b.slots, replace, 0)
    put_back(b, r, r.out, r.result, r.out_tiles)


def put_back(b, r, values, target, tiles):
    tile = tiles.shape[1]

    def body(step, carry):
        first = pl.multiple_of(step * tile, tile)
        chosen = low((iota((tile, b.tokens), 0) + first == r.index[0:1, :]).astype(F32))
        copy = pltpu.make_async_copy(tiles.at[0], target.at[pl.ds(first, tile), :], r.sem)
        tiles[0] = nt(chosen, values[...]).astype(target.dtype)
        copy.start()
        copy.wait()
        return carry

    lax.fori_loop(0, b.rows // tile, body, 0)


def backward_mlp(b, r):
    chunk = 256 if b.hidden % 512 == 0 else b.hidden // 4
    half = b.hidden // 2
    r.sums[...] = jnp.zeros_like(r.sums)

    def body(slot, carry):
        cols = slot_columns(b, slot)
        z_grad = r.z[:, cols]
        z_low = low(z_grad)
        r.zg[:, cols] = z_low
        for part in range(2):
            for at in range(0, half, chunk):
                here = part * half + at
                active = nn(r.down[part][at : at + chunk, :], z_low)
                r.g[here : here + chunk, cols] = low(
                    active * r.g[here : here + chunk, cols].astype(F32)
                )
        grad = nn(r.up[0][...], r.g[0:half, cols]) + nn(r.up[1][...], r.g[half:, cols])
        unit, scale = norm(r.y[:, cols], 0)
        ones = jnp.ones((16, b.width), BF16)
        r.sums[0] += nt(ones, low(grad))
        r.sums[1] += nt(ones, low(grad * unit))
        grad = z_grad + norm_back(grad * r.gainT[:, 1:2], unit, scale, 0)
        r.z[:, cols] = grad
        y_low = low(grad)
        r.yg[:, cols] = y_low
        r.og[:, cols] = low(nn(r.w_out[...], y_low))
        return carry

    lax.fori_loop(0, b.slots, body, 0)
    r.table[1:2, :] = r.sums[1, 0:1, :]
    r.table[5 + 4 : 5 + 5, :] = r.sums[0, 0:1, :]


def backward_attention(b, r):
    columns, head, width = b.columns, b.head, b.width
    factor = float(head) ** (-0.5)
    r.sums[...] = jnp.zeros_like(r.sums)

    def body(slot, carry):
        cols = slot_columns(b, slot)
        mask = slot_mask(b, slot)
        for h in range(HEADS):
            at_q = slice(h * head, (h + 1) * head)
            at_k = slice(columns + h * head, columns + (h + 1) * head)
            at_v = slice(2 * columns + h * head, 2 * columns + (h + 1) * head)
            q, k, v = r.qkv[at_q, cols], r.qkv[at_k, cols], r.qkv[at_v, cols]
            o_grad = r.og[at_q, cols]
            wide = jnp.exp2(tn(k, q) * (factor * LOG2E) + (mask - r.logs[h : h + 1, cols]))
            chances = low(wide)
            chance_grad = tn(v, o_grad)
            inner = jnp.sum(chance_grad * wide, 0, keepdims=True)
            score_grad = low(wide * ((chance_grad - inner) * factor))
            r.qkv[at_q, cols] = low(nn(k, score_grad))
            r.qkv[at_k, cols] = low(nt(q, score_grad))
            r.qkv[at_v, cols] = low(nt(o_grad, chances))
        grad = nn(r.w_in[...], r.qkv[:, cols])
        unit, scale = norm(r.x[:, cols].astype(F32), 0)
        ones = jnp.ones((16, b.width), BF16)
        r.sums[0] += nt(ones, low(grad))
        r.sums[1] += nt(ones, low(grad * unit))
        r.x[:, cols] = low(r.z[:, cols] + norm_back(grad * r.gainT[:, 0:1], unit, scale, 0))
        return carry

    lax.fori_loop(0, b.slots, body, 0)
    r.table[0:1, :] = r.sums[1, 0:1, :]
    r.table[5:6, :] = r.sums[0, 0:1, :]


class Place:
    def __init__(self, small, large):
        ds, dl = small.columns, large.columns
        self.first, self.size, at = {}, {}, 0
        for name, rows in (
            ("small_up", ds), ("small_down", ds), ("large_up", 2 * dl), ("large_down", 2 * dl), ("bias", 16),
            ("other", 2 * ds + 4 * dl + 16),
            ("large_cross", 4 * dl), ("small_cross", 2 * ds), ("small_enter", ds), ("small_leave", ds),
            ("large_enter", ds), ("large_leave", ds),
            ("large_heads", 4 * dl), ("small_heads", 2 * ds), ("tables", 64),
        ):
            self.first[name], self.size[name] = at, rows
            at += rows
        self.total = at

    def rows(self, name, part=0, size=None):
        first = self.first[name] + part
        return slice(first, first + (self.size[name] if size is None else size))


class CrossGrads:
    def __init__(self, own, other, place, buffer):
        self.own, self.other, self.place, self.buffer = own, other, place, buffer
        self.kept = {}

    def put(self, name, part, values):
        first = self.place.first[name] + part
        self.buffer[first : first + values.shape[0], :] = low(values)

    def cross_in(self, third, values):
        if self.other.index == 1:
            self.put("large_cross", third * self.other.columns, values)
            return
        self.kept[third] = values
        if third == 1:
            self.put("small_cross", 0, jnp.concatenate([self.kept[0], values], 1))
        if third == 2:
            self.put(
                "small_cross", self.other.columns, jnp.concatenate([values, self.kept["out"]], 1)
            )

    def cross_out(self, values):
        if self.other.index == 1:
            self.put("large_cross", 3 * self.other.columns, values)
        else:
            self.kept["out"] = values

    def enter(self, values):
        if self.own.index == 0:
            self.put("small_enter", 0, values)
        else:
            self.put("large_enter", 0, side_by_side(values))

    def leave(self, values):
        if self.own.index == 1:
            self.put("large_leave", 0, values)
        else:
            self.put("small_leave", 0, side_by_side(values))


def side_by_side(values):
    half = values.shape[0] // 2
    return jnp.concatenate([values[:half], values[half:]], 1)


def mlp_grads(b, r, place, buffer):
    half, columns = b.hidden // 2, b.columns
    name = ("small", "large")[b.index]
    r.table[5 + 5 : 5 + 6, :] = nt(r.u[b.hidden : b.hidden + 16, :], r.zg[...])[0:1]
    for part in range(2):
        base = place.first["other"] * part
        mine = slice(part * half, (part + 1) * half)
        up = nt(r.c[...], r.g[mine, :])
        first = base + place.first[name + "_up"]
        for at in range(0, half, LANES):
            buffer[first : first + columns, :] = low(up[0:columns, at : at + LANES])
            first += columns
        bias_row = base + place.first["bias"]
        bias = low(up[columns : columns + 16, :])
        first = base + place.first[name + "_down"]
        down = nt(r.u[mine, :], r.zg[...])
        if b.index == 0:
            buffer[first : first + columns, :] = low(side_by_side(down))
            r.bias_rows[part, 0:1, :] = bias[0:1, :].astype(F32)
        else:
            buffer[first : first + half, :] = low(down)
            r.bias_rows[part, 1:2, :] = bias[0:1, 0:LANES].astype(F32)
            r.bias_rows[part, 2:3, :] = bias[0:1, LANES:].astype(F32)


def bias_rows(rows, place, buffer):
    for part in range(2):
        first = place.first["other"] * part + place.first["bias"]
        buffer[first : first + 16, :] = low(rows[part])


def head_grads(b, r, place, buffer):
    columns = b.columns
    w_in = nt(r.a[...], r.qkv[...])
    w_out = nt(r.o[...], r.yg[...])
    r.table[5 + 1 : 5 + 2, :] = w_in[columns : columns + 1, 0:columns]
    r.table[5 + 2 : 5 + 3, :] = w_in[columns : columns + 1, 2 * columns : 3 * columns]
    r.table[5 + 3 : 5 + 4, :] = w_out[columns : columns + 1, :]
    if b.index == 1:
        first = place.first["large_heads"]
        for third in range(3):
            buffer[first : first + columns, :] = low(
                w_in[0:columns, third * columns : (third + 1) * columns]
            )
            first += columns
        buffer[first : first + columns, :] = low(w_out[0:columns])
    else:
        first = place.first["small_heads"]
        buffer[first : first + columns, :] = low(w_in[0:columns, 0:LANES])
        buffer[first + columns : first + 2 * columns, :] = low(
            jnp.concatenate([w_in[0:columns, LANES:], w_out[0:columns]], 1)
        )


NAMES = (
    "counts", "small_rows", "large_rows", "small_cot", "large_cot",
    "small_in", "small_out", "small_up", "small_up_bias", "small_down",
    "large_in", "large_out", "large_up", "large_up_bias", "large_down",
    "small_enter", "large_cross_in", "large_cross_out", "small_leave",
    "large_enter", "small_cross_in", "small_cross_out", "large_leave",
    "small_gains", "small_shifts", "large_gains", "large_shifts",
    "other_small_up", "other_small_up_bias", "other_small_down",
    "other_large_up", "other_large_up_bias", "other_large_down",
)


def scratch_of(b):
    d, t, h = b.columns, b.tokens, b.hidden
    return dict(
        logs=pltpu.VMEM((8, t), F32),
        out_tiles=pltpu.VMEM((2, 256, d), BF16),
        grad_tiles=pltpu.VMEM((2, 256, d), F32),
        sem=pltpu.SemaphoreType.DMA(()),
        index=pltpu.VMEM((8, t), jnp.int32),
        x=pltpu.VMEM((d, t), BF16),
        cotT=pltpu.VMEM((d, t), BF16),
        a=pltpu.VMEM((d + 16, t), BF16),
        qkv=pltpu.VMEM((3 * d, t), BF16),
        o=pltpu.VMEM((d + 16, t), BF16),
        y=pltpu.VMEM((d, t), F32),
        c=pltpu.VMEM((d + 16, t), BF16),
        u=pltpu.VMEM((h + 16, t), BF16),
        g=pltpu.VMEM((h, t), BF16),
        z=pltpu.VMEM((d, t), F32),
        n=pltpu.VMEM((d, t), BF16),
        og=pltpu.VMEM((d, t), BF16),
        sp=pltpu.VMEM((2 * STACK, t), BF16),
        maps=pltpu.VMEM((2 * STACK, d), BF16),
        cls=pltpu.VMEM((CLS, d), F32),
        cot_cls=pltpu.VMEM((CLS, d), F32),
        new_cls=pltpu.VMEM((CLS, d), BF16),
        cls_grad=pltpu.VMEM((CLS, d), F32),
        sums=pltpu.VMEM((2, 16, d), F32),
        table=pltpu.VMEM((24, d), F32),
        gainT=pltpu.VMEM((d, 128), F32),
        shiftT=pltpu.VMEM((d, 128), F32),
        up_biasT=pltpu.VMEM((h, 128), F32),
        w_inT=pltpu.VMEM((3 * d, d), BF16),
        w_outT=pltpu.VMEM((d, d), BF16),
        w_upT=pltpu.VMEM((h, d), BF16),
        w_downT=pltpu.VMEM((d, h), BF16),
    )


def columns_of(rows):
    rows = rows.astype(F32)
    return jnp.concatenate([rows, jnp.zeros((128 - rows.shape[0], rows.shape[1]), F32)], 0).T


def prepare(b, r):
    r.gainT[...] = columns_of(r.gains[...])
    r.shiftT[...] = columns_of(r.shifts[...])
    half = b.hidden // 2
    for part in range(2):
        r.up_biasT[part * half : (part + 1) * half, :] = columns_of(r.up_bias[part][...])
        r.w_upT[part * half : (part + 1) * half, :] = r.up[part][...].T
        r.w_downT[:, part * half : (part + 1) * half] = r.down[part][...].T
    r.w_inT[...] = r.w_in[...].T
    r.w_outT[...] = r.w_out[...].T
    r.a[b.columns : b.columns + 16, :] = jnp.ones((16, b.tokens), BF16)
    r.o[b.columns : b.columns + 16, :] = jnp.ones((16, b.tokens), BF16)
    r.c[b.columns : b.columns + 16, :] = jnp.ones((16, b.tokens), BF16)
    r.u[b.hidden : b.hidden + 16, :] = jnp.ones((16, b.tokens), BF16)
    r.table[...] = jnp.zeros_like(r.table)


class Refs:
    pass


def layer_kernel(small, large, place, keys, *refs):
    ins = dict(zip(NAMES, refs))
    refs = refs[len(NAMES) :]
    small_out, large_out, small_grad, large_grad, buffer = refs[:5]
    refs = refs[5:]
    groups = []
    for b, name, result, grad in (
        (small, "small", small_out, small_grad),
        (large, "large", large_out, large_grad),
    ):
        r = Refs()
        for key in keys:
            setattr(r, key, refs[0])
            refs = refs[1:]
        r.rows, r.cot = ins[name + "_rows"], ins[name + "_cot"]
        r.w_in, r.w_out = ins[name + "_in"], ins[name + "_out"]
        r.up = (ins[name + "_up"], ins["other_" + name + "_up"])
        r.down = (ins[name + "_down"], ins["other_" + name + "_down"])
        r.up_bias = (ins[name + "_up_bias"], ins["other_" + name + "_up_bias"])
        r.gains, r.shifts = ins[name + "_gains"], ins[name + "_shifts"]
        r.enter, r.leave = ins[name + "_enter"], ins[name + "_leave"]
        r.cross_in, r.cross_out = ins[name + "_cross_in"], ins[name + "_cross_out"]
        r.result, r.grad = result, grad
        r.stack = r.g.at[0 : 2 * b.columns, 0 : b.rows]
        r.out, r.zg, r.yg = r.og, r.n, r.cotT
        groups.append((b, r))
    biases = refs[0]
    (bs, rs), (bl, rl) = groups
    rs.bias_rows = rl.bias_rows = biases
    biases[...] = jnp.zeros_like(biases)
    for b, r in groups:
        prepare(b, r)
        lay_out(b, r, ins["counts"])
        bring_in(b, r)
    for b, r in groups:
        forward_attention(b, r)
    for b, r in groups:
        forward_mlp(b, r)
    cross(bs, rs, bl, rl, CrossGrads(bs, bl, place, buffer))
    cross(bl, rl, bs, rs, CrossGrads(bl, bs, place, buffer))
    for b, r in groups:
        backward_cross(b, r)
        put_out(b, r)
    for b, r in groups:
        backward_mlp(b, r)
        mlp_grads(b, r, place, buffer)
    bias_rows(biases, place, buffer)
    for b, r in reversed(groups):
        backward_attention(b, r)
        head_grads(b, r, place, buffer)
        put_back(b, r, r.x, r.grad, r.grad_tiles)
    first = place.first["tables"]
    buffer[first : first + 32, :] = jnp.concatenate(
        [low(rl.table[...]), jnp.zeros((8, LANES), BF16)], 0
    )
    buffer[first + 32 : first + 64, :] = jnp.concatenate(
        [
            jnp.concatenate([low(rs.table[...]), jnp.zeros((8, small.columns), BF16)], 0),
            jnp.zeros((32, LANES - small.columns), BF16),
        ],
        1,
    )


def run_layer(args):
    rows_s, rows_l = args[1].shape[0], args[2].shape[0]
    small = Branch(0, rows_s, args[1].shape[1], 2 * args[7].shape[1], 256, ((0, 4), (1, 5), (2,), (3,), (6,)))
    large = Branch(1, rows_l, args[2].shape[1], 2 * args[12].shape[1], 384, ((0, 1, 4), (2, 3, 5), (6,)))
    place = Place(small, large)
    keys = tuple(scratch_of(small))
    scratch = [s for b in (small, large) for s in scratch_of(b).values()]
    scratch.append(pltpu.VMEM((2, 16, LANES), F32))
    vmem = pl.BlockSpec(memory_space=pltpu.VMEM)
    return pl.pallas_call(
        functools.partial(layer_kernel, small, large, place, keys),
        out_shape=(
            jax.ShapeDtypeStruct(args[1].shape, BF16),
            jax.ShapeDtypeStruct(args[2].shape, BF16),
            jax.ShapeDtypeStruct(args[1].shape, F32),
            jax.ShapeDtypeStruct(args[2].shape, F32),
            jax.ShapeDtypeStruct((place.total, LANES), BF16),
        ),
        in_specs=[pl.BlockSpec(memory_space=pltpu.SMEM)] + [vmem] * (len(NAMES) - 1),
        out_specs=(pl.BlockSpec(memory_space=pl.ANY),) * 4 + (vmem,),
        scratch_shapes=scratch,
        compiler_params=pltpu.CompilerParams(vmem_limit_bytes=VMEM_LIMIT),
        name="layer",
    )(*args), place


def matrix(buffer, first, rows, count):
    parts = [buffer[first + i * rows : first + (i + 1) * rows] for i in range(count)]
    return jnp.concatenate(parts, 1) if count > 1 else parts[0]


def stacked(values):
    half = values.shape[1] // 2
    return jnp.concatenate([values[:, :half], values[:, half:]], 0)


def shards(*args):
    (
        small_rows, large_rows, counts, small_cot, large_cot,
        small_in, small_out, small_up, small_up_bias, small_down,
        large_in, large_out, large_up, large_up_bias, large_down,
    ) = args[:15]
    mine = (
        small_up, small_up_bias[None], small_down, large_up, large_up_bias[None], large_down,
    )
    theirs = tuple(lax.ppermute(value, "tensor", [(0, 1), (1, 0)]) for value in mine)
    inputs = (
        counts, small_rows, large_rows, small_cot, large_cot,
        small_in, small_out, small_up, mine[1], small_down,
        large_in, large_out, large_up, mine[4], large_down,
    ) + args[15:] + theirs
    (small_result, large_result, small_grad, large_grad, buffer), place = run_layer(inputs)
    other = place.first["other"]
    mlp = buffer[:other] + lax.ppermute(buffer[other : 2 * other], "tensor", [(0, 1), (1, 0)])
    mlp = lax.psum(mlp, "dp").astype(F32)
    rest = lax.psum(buffer[2 * other :], ("dp", "tensor")).astype(F32)
    first = {key: value - 2 * other for key, value in place.first.items()}
    ds, dl = small_rows.shape[1], large_rows.shape[1]
    cross_l = matrix(rest, first["large_cross"], dl, 4)
    cross_s = matrix(rest, first["small_cross"], ds, 2)
    heads_l = matrix(rest, first["large_heads"], dl, 4)
    heads_s = matrix(rest, first["small_heads"], ds, 2)
    tables = rest[first["tables"] :]
    bias = mlp[place.first["bias"] :]
    place = place.first
    return (
        small_result,
        large_result,
        small_grad,
        large_grad,
        heads_s[:, : 3 * ds],
        heads_s[:, 3 * ds :],
        matrix(mlp, place["small_up"], ds, 1),
        bias[0],
        stacked(mlp[place["small_down"] : place["small_down"] + ds]),
        heads_l[:, : 3 * dl],
        heads_l[:, 3 * dl :],
        matrix(mlp, place["large_up"], dl, 2),
        bias[1:3].reshape(-1),
        mlp[place["large_down"] : place["large_down"] + 2 * dl],
        matrix(rest, first["small_enter"], ds, 1),
        cross_l[:, : 3 * dl],
        cross_l[:, 3 * dl :],
        stacked(matrix(rest, first["small_leave"], ds, 1)),
        stacked(matrix(rest, first["large_enter"], ds, 1)),
        cross_s[:, : 3 * ds],
        cross_s[:, 3 * ds :],
        matrix(rest, first["large_leave"], ds, 1),
        tables[32:37, :ds],
        tables[37:51, :ds],
        tables[0:5],
        tables[5:19],
    )


def solution(mesh):
    both = ("dp", "tensor")
    rows = P(both, None)
    mlp = (P(None, "tensor"), P("tensor"), P("tensor", None))
    return jax.shard_map(
        shards,
        mesh=mesh,
        in_specs=(rows, rows, P(None, both), rows, rows)
        + ((P(), P()) + mlp) * 2
        + (P(),) * 12,
        out_specs=(rows,) * 4 + ((P(), P()) + mlp) * 2 + (P(),) * 12,
        check_vma=False,
    )
```

time: 990 us -> 447 us (0.45)
  matrix products: 493 us -> 0 us
  waiting for transfers between devices: 102 us -> 242 us
  Pallas kernels: 0 us -> 129 us
  local copies, waits for them, and re-layouts: 147 us -> 40.9 us
  other arithmetic: 113 us -> 7.07 us
  blocking collectives: 101 us -> 0 us
    dot_general x94 -> x0, matrix products: 493 us -> none  [the longest x4 120 us: one_block(): jnp.einsum('hqk,khd->qhd', grad_scores, all_keys, preferred_element_type=...]
    pallas_call x0 -> x1, Pallas kernels: none -> 129 us  [run_layer(): pl.pallas_call(functools.partial(layer_kernel, small, large, place, keys)...]
    psum x2, waiting for transfers between devices: 67.4 us -> 184 us  [the longest x1 103 us: shards(): rest = lax.psum(buffer[2 * other:], ('dp', 'tensor')).astype(F32)]
    psum x2 -> x0, blocking collectives: 74.3 us -> none  [the longest x1 38.6 us: shards(): lax.psum((grad_small_heads_in, grad_small_heads_out, grad_large_heads_in,...]
    reduce_sum x56 -> x0, other arithmetic: 61.7 us -> none  [the longest x12 17.4 us: layer_norm(): return center * lax.rsqrt(spread + EPSILON) * gain + shift]
    ppermute x0 -> x7, waiting for transfers between devices: none -> 58 us  [the longest x1 31.5 us: shards(): lax.ppermute(buffer[other:2 * other], 'tensor', [(0, 1), (1, 0)])]
    unnamed x682 -> x30, local copies, waits for them, and re-layouts: 47.6 us -> 16.4 us
    all_gather x2 -> x0, blocking collectives: 27.1 us -> none  [the longest x1 14.3 us: mlp_backward(): grad_rows = lax.all_gather(out_low, 'tensor', axis=0, tiled=True)]
  transfers between devices with their start and end apart: 8 -> 9, of which waited for: 3 -> 4; matrix products, arithmetic and copies ran while one was open for 54% -> 8% of each run, Pallas kernels for 0% -> 0%
where the time goes in v1:
time: 447 us; the launch traced here: 443 us
  waiting for transfers between devices  242 us (54%)
  Pallas kernels  129 us (29%)
  local copies, waits for them, and re-layouts  40.9 us (9%)
  between operations  14.6 us (3%)
  starting transfers between devices  9.25 us (2%)
  other arithmetic  7.07 us (2%)
    pallas_call x1, Pallas kernels, run_layer(): pl.pallas_call(functools.partial(layer_kernel, small, large, place, keys)...  129 us
    psum x1, waiting for transfers between devices, shards(): rest = lax.psum(buffer[2 * other:], ('dp', 'tensor')).astype(F32)  103 us
    psum x1, waiting for transfers between devices, shards(): mlp = lax.psum(mlp, 'dp').astype(F32)  80.6 us
    ppermute x1, waiting for transfers between devices, shards(): lax.ppermute(buffer[other:2 * other], 'tensor', [(0, 1), (1, 0)])  31.5 us
    ppermute x6, waiting for transfers between devices, shards(): lax.ppermute(value, 'tensor', [(0, 1), (1, 0)])  26.5 us
    unnamed x30, local copies, waits for them, and re-layouts  16.4 us
  transfers between devices with their start and end apart: 9, of which 4 were waited for; matrix products, arithmetic and copies ran while one was open for 8% of the time, Pallas kernels for 0%

profile of v1, /device:TPU:0, one launch (start us, length us, event | category | flops | bytes accessed | tf_op | source)
XLA Modules:
  0.0 443.2 jit_solution(5080001560584010731)
XLA Ops:
  7.3 3.0 collective-permute-start.3
  10.3 0.1 collective-permute-start.5
  10.4 1.9 collective-permute-start
  12.3 1.0 copy.56.refs_9_
  13.4 0.7 copy-done.1
  14.0 0.1 collective-permute-start.2
  14.1 0.7 broadcast_in_dim.6.refs_8_
  14.8 1.9 collective-permute-start.1
  16.8 0.7 broadcast_in_dim.7.refs_13_
  17.4 26.5 %collective-permute-done.1.refs_28_ = bf16[1,384]{1,0:T(2,128)(2,1)S(1)} collective-permute-done((bf16[1,384]{1,0:T(2,128)(2,1)S(1)}, bf16[1,384]{1,0:T(2,128)(2,1)S(1)}, u32[]{:S(2)}, u32[]{:S(2)}) %collective-permute-start.1) | collective-permute-done | bytes 800 | tf_op jit(solution)/shard_map/ppermute | solution.py:791
  43.9 0.6 copy-done.9
  44.5 1.7 collective-permute-start.4
  46.2 1.7 copy.57.refs_18_
  47.9 1.7 copy.58.refs_19_
  49.7 2.0 copy.54.refs_1_
  51.7 1.0 copy.55.refs_3_
  52.7 0.7 copy-done.4
  53.4 129.3 %layer.1 = (bf16[1024,192]{1,0:T(8,128)(2,1)}, bf16[1024,384]{1,0:T(8,128)(2,1)}, f32[1024,192]{1,0:T(8,128)}, f32[1024,384]{1,0:T(8,128)}, bf16[8544,384]{1,0:T(8,128)(2,1)}) custom-call(s32[2,6]{1,0:T(2,128)} %refs_0_.1, bf16[1024,192]{1,0:T(8,128)(2,1)} %copy.54.refs_1_, bf16[1024,384]{1,0:T(8,128)(2,1)} %refs_2_.1, bf16[1024,192]{1,0:T(8,128)(2,1)} %copy.55.refs_3_, ...), custom_call_target="tpu_custom_call" | custom-call | tf_op jit(solution)/shard_map/layer/pallas_call | solution.py:755
  182.8 1.5 slice.136
  184.3 0.4 collective-permute-start.6
  184.7 4.3 slice.130
  189.0 1.0 copy-done.2
  190.0 0.9 copy.59
  190.9 2.4 copy.60
  193.3 31.5 %collective-permute-done.6 = bf16[1936,384]{1,0:T(8,128)(2,1)S(1)} collective-permute-done((bf16[1936,384]{1,0:T(8,128)(2,1)S(1)}, bf16[1936,384]{1,0:T(8,128)(2,1)S(1)}, u32[]{:S(2)}, u32[]{:S(2)}) %collective-permute-start.6) | collective-permute-done | bytes 1486880 | tf_op jit(solution)/shard_map/ppermute | solution.py:799
  224.9 2.7 slice_add_fusion
  227.6 103.3 %all-reduce.3.cloned.1.call-done = bf16[4672,384]{1,0:T(8,128)(2,1)} async-done(((bf16[4672,384]{1,0:T(8,128)(2,1)}), bf16[4672,384]{1,0:T(8,128)(2,1)}) %all-reduce.3.cloned.1.call-update) | async-done | bytes 3588112 | tf_op jit(solution)/shard_map/psum | solution.py:801
  330.9 2.2 fusion
  333.1 1.0 pad_maximum_fusion.3
  334.1 2.0 fusion.1
  336.2 0.9 copy.62
  337.1 0.9 copy.63
  337.9 1.3 slice.195
  339.2 1.3 slice.197
  340.5 1.3 slice.196
  341.8 1.3 slice.198
  343.2 2.9 fusion.2
  346.1 2.0 pad_maximum_fusion
  348.1 80.6 %all-reduce.5.cloned.1.call-done = bf16[1936,384]{1,0:T(8,128)(2,1)} async-done(((bf16[1936,384]{1,0:T(8,128)(2,1)}), bf16[1936,384]{1,0:T(8,128)(2,1)}) %all-reduce.5.cloned.1.call-update) | async-done | bytes 1486864 | tf_op jit(solution)/shard_map/psum | solution.py:800
  428.7 0.8 slice.180
  429.5 0.6 reshape.55
  430.1 1.1 fusion.4
  431.2 0.9 copy.61
  432.1 0.2 convert_element_type.7
  432.3 0.6 slice_reduce_fusion
  433.0 1.1 pad_maximum_fusion.2
  434.1 0.7 slice.170
  434.8 1.1 slice.181
  (28 shorter events, 0.3 us)
Async XLA Ops:
  7.2 44.4 %copy-start.3 = (bf16[1024,192]{0,1:T(8,128)(2,1)S(1)}, bf16[1024,192]{0,1:T(8,128)(2,1)}, u32[]{:S(2)}) copy-start(bf16[1024,192]{0,1:T(8,128)(2,1)} %param.30) | copy-start | bytes 1179652
  7.2 323.7 %all-reduce.3.cloned.1.call-start = ((), (), s32[]{:S(2)}) async-start(), calls=%async_computation | async-start | bytes 7176192 | tf_op jit(solution)/shard_map/psum | solution.py:801
  7.3 46.1 %collective-permute-start.3 = (bf16[384,768]{1,0:T(8,128)(2,1)}, bf16[384,768]{1,0:T(8,128)(2,1)}, u32[]{:S(2)}, u32[]{:S(2)}) collective-permute-start(bf16[384,768]{1,0:T(8,128)(2,1)} %refs_12_.1), channel_id=1, source_target_pairs={{0,1},{1,0},{2,3},{3,2},{4,5},{5,4},{6,7},{7,6},{8,9},{9,8},{10,11... | collective-permute-start | bytes 1769480 | tf_op jit(solution)/shard_map/ppermute | solution.py:791
  10.3 43.1 %collective-permute-start.5 = (bf16[768,384]{1,0:T(8,128)(2,1)}, bf16[768,384]{1,0:T(8,128)(2,1)}, u32[]{:S(2)}, u32[]{:S(2)}) collective-permute-start(bf16[768,384]{1,0:T(8,128)(2,1)} %refs_14_.1), channel_id=1, source_target_pairs={{0,1},{1,0},{2,3},{3,2},{4,5},{5,4},{6,7},{7,6},{8,9},{9,8},{10,11... | collective-permute-start | bytes 1769480 | tf_op jit(solution)/shard_map/ppermute | solution.py:791
  10.4 42.3 %collective-permute-start = (bf16[192,384]{1,0:T(8,128)(2,1)}, bf16[192,384]{1,0:T(8,128)(2,1)S(1)}, u32[]{:S(2)}, u32[]{:S(2)}) collective-permute-start(bf16[192,384]{1,0:T(8,128)(2,1)} %refs_7_.1), channel_id=1, source_target_pairs={{0,1},{1,0},{2,3},{3,2},{4,5},{5,4},{6,7},{7,6},{8,9},{9,8},{10,11... | collective-permute-start | bytes 442376 | tf_op jit(solution)/shard_map/ppermute | solution.py:791
  13.4 0.7 copy-start.1
  14.0 38.6 %collective-permute-start.2 = (bf16[384,192]{1,0:T(8,128)(2,1)S(1)}, bf16[384,192]{1,0:T(8,128)(2,1)S(1)}, u32[]{:S(2)}, u32[]{:S(2)}) collective-permute-start(bf16[384,192]{1,0:T(8,128)(2,1)S(1)} %copy.56.refs_9_), channel_id=1, source_target_pairs={{0,1},{1,0},{2,3},{3,2},{4,5},{5,4},{6,7},{7,6},{8,9},{9,8},{10,11... | collective-permute-start | bytes 442376 | tf_op jit(solution)/shard_map/ppermute | solution.py:791
  14.8 2.6 copy-start.7
  14.8 29.1 %collective-permute-start.1 = (bf16[1,384]{1,0:T(2,128)(2,1)S(1)}, bf16[1,384]{1,0:T(2,128)(2,1)S(1)}, u32[]{:S(2)}, u32[]{:S(2)}) collective-permute-start(bf16[1,384]{1,0:T(2,128)(2,1)S(1)} %broadcast_in_dim.6.refs_8_), channel_id=1, source_target_pairs={{0,1},{1,0},{2,3},{3,2},{4,5},{5,4},{6,7},{7,6},{8,9},{9,8},{10,11... | collective-permute-start | bytes 2312 | tf_op jit(solution)/shard_map/ppermute | solution.py:791
  17.4 36.0 %copy-start.6 = (bf16[1,768]{1,0:T(2,128)(2,1)}, bf16[1,768]{1,0:T(2,128)(2,1)S(1)}, u32[]{:S(2)}) copy-start(bf16[1,768]{1,0:T(2,128)(2,1)S(1)} %broadcast_in_dim.7.refs_13_) | copy-start | bytes 4612
  43.9 0.6 copy-start.9
  44.5 8.2 %collective-permute-start.4 = (bf16[1,768]{1,0:T(2,128)(2,1)S(1)}, bf16[1,768]{1,0:T(2,128)(2,1)S(1)}, u32[]{:S(2)}, u32[]{:S(2)}) collective-permute-start(bf16[1,768]{1,0:T(2,128)(2,1)S(1)} %broadcast_in_dim.7.refs_13_), channel_id=1, source_target_pairs={{0,1},{1,0},{2,3},{3,2},{4,5},{5,4},{6,7},{7,6},{8,9},{9,8},{10,11... | collective-permute-start | bytes 4616 | tf_op jit(solution)/shard_map/ppermute | solution.py:791
  52.7 0.7 copy-start.8
  52.7 0.7 copy-start.5
  52.7 0.7 copy-start.4
  184.3 40.6 %collective-permute-start.6 = (bf16[1936,384]{1,0:T(8,128)(2,1)S(1)}, bf16[1936,384]{1,0:T(8,128)(2,1)S(1)}, u32[]{:S(2)}, u32[]{:S(2)}) collective-permute-start(bf16[1936,384]{1,0:T(8,128)(2,1)S(1)} %slice.136), channel_id=1, source_target_pairs={{0,1},{1,0},{2,3},{3,2},{4,5},{5,4},{6,7},{7,6},{8,9},{9,8},{10,11... | collective-permute-start | bytes 4460552 | tf_op jit(solution)/shard_map/ppermute | solution.py:799
  188.9 1.0 copy-start.2
  189.0 239.7 %all-reduce.5.cloned.1.call-start = ((), (), s32[]{:S(2)}) async-start(), calls=%async_computation.1 | async-start | bytes 2973696 | tf_op jit(solution)/shard_map/psum | solution.py:800
  428.7 3.4 copy-start
Sparse Core Ops, SparseCore 0:
  189.1 141.7 all-reduce.2
  334.8 93.8 all-reduce.4
